TPU v7x, 256 devices: a whole 4x4x8 slice. The times are simulated.
256 devices in a mesh: tm: 16 (over x, y_lo, core), patch: 16 (over z, y_hi).
Axes of the slice: x: 4, y: 4 (y_hi: 2, y_lo: 2; y = y_hi * 2 + y_lo), z: 8, core: 2. Of those that a mesh axis runs over, the one named last changes fastest.
Arguments:
- queries: bfloat16 [1, 64, 1024, 1024], P(None, 'tm', 'patch'), may hold values from -36 to 36
- key_vectors: bfloat16 [1, 64, 1024, 1024], P(None, 'tm', 'patch'), may hold values from -36 to 36
- value_vectors: bfloat16 [1, 64, 1024, 1024], P(None, 'tm', 'patch'), may hold values from -6 to 6
- grad_output: bfloat16 [1, 64, 1024, 1024], P(None, 'tm', 'patch'), may hold values from -6 to 6
- window_start: int32 [64], replicated, may hold values from 0 to 48, as said below
Outputs:
- attended: bfloat16 [1, 64, 1024, 1024], P(None, 'tm', 'patch')
- grad_queries: bfloat16 [1, 64, 1024, 1024], P(None, 'tm', 'patch')
- grad_keys: bfloat16 [1, 64, 1024, 1024], P(None, 'tm', 'patch')
- grad_values: bfloat16 [1, 64, 1024, 1024], P(None, 'tm', 'patch')
Inputs may be any that keep to these rules, and one draw needn't show every extreme that they name: Frame f lies in frames window_start[f] to window_start[f] + 15, and these lie within the clip.
All inputs are finite; a program needn't handle non-finite values.
Results may differ from a plain program's by a relative error of at most 0.015.
Values may be sent and summed in bfloat16 or wider, within the bound.
A program may use at most 128 MiB of HBM per device.

v0:
```python
import jax
import jax.numpy as jnp
from jax import lax
from jax.sharding import PartitionSpec as P

HD = 64
WINDOW = 16


def from_behind(array, axis, by):
    devices = lax.axis_size(axis)
    pairs = [(i, i + by) for i in range(devices) if 0 <= i + by < devices]
    return lax.ppermute(array, axis, pairs)


def attention_core(queries, key_rows, value_rows, grad_rows, allowed):
    scaling = queries.shape[-1] ** (-0.5)
    scores = (
        jnp.einsum("bqphd,bkphd->bphqk", queries, key_rows, preferred_element_type=jnp.float32)
        * scaling
    )
    if allowed is not None:
        scores = jnp.where(allowed, scores, -1e30)
    highest = jnp.max(scores, axis=-1, keepdims=True)
    exponent = jnp.exp(scores - highest)
    weights = exponent / jnp.sum(exponent, axis=-1, keepdims=True)
    weights_b = weights.astype(jnp.bfloat16)
    attended = jnp.einsum(
        "bphqk,bkphd->bqphd", weights_b, value_rows, preferred_element_type=jnp.float32
    ).astype(jnp.bfloat16)
    weight_grad = jnp.einsum(
        "bqphd,bkphd->bphqk", grad_rows, value_rows, preferred_element_type=jnp.float32
    )
    score_grad = weights * (weight_grad - jnp.sum(weights * weight_grad, axis=-1, keepdims=True))
    score_grad_b = score_grad.astype(jnp.bfloat16)
    grad_queries = (
        jnp.einsum("bphqk,bkphd->bqphd", score_grad_b, key_rows, preferred_element_type=jnp.float32)
        * scaling
    )
    grad_keys = (
        jnp.einsum("bphqk,bqphd->bkphd", score_grad_b, queries, preferred_element_type=jnp.float32)
        * scaling
    )
    grad_values = jnp.einsum(
        "bphqk,bqphd->bkphd", weights_b, grad_rows, preferred_element_type=jnp.float32
    )
    return (attended, grad_queries, grad_keys, grad_values)


def window_mask(key_frames, starts):
    return (key_frames[None, :] >= starts[:, None]) & (
        key_frames[None, :] < starts[:, None] + WINDOW
    )


def on_device(queries, key_vectors, value_vectors, grad_output, window_start):
    clip_count, frames_dev, patches_dev, width = queries.shape
    half_width = width // 2
    head_size = HD
    group_width = 2 * head_size
    groups = half_width // group_width
    temporal_heads = half_width // head_size
    patch_devices = lax.axis_size("patch")

    def to_items(tensor):
        spatial = tensor[..., :half_width].reshape(
            clip_count, frames_dev, patches_dev, groups, group_width
        )
        return spatial.transpose(0, 1, 3, 2, 4).reshape(patch_devices, -1, patches_dev, group_width)

    def from_items(tensor):
        shaped = tensor.reshape(clip_count, frames_dev, groups, patches_dev, group_width)
        return shaped.transpose(0, 1, 3, 2, 4).reshape(
            clip_count, frames_dev, patches_dev, half_width
        )

    def one_item(item):
        shaped = [part.reshape(1, part.shape[0], 1, 2, head_size) for part in item]
        results = attention_core(shaped[0], shaped[1], shaped[2], shaped[3], None)
        return tuple(
            (
                result.astype(jnp.bfloat16).reshape(result.shape[1], group_width)
                for result in results
            )
        )

    results = lax.map(
        one_item,
        (
            lax.all_to_all(to_items(queries), "patch", split_axis=0, concat_axis=2, tiled=True)[0],
            lax.all_to_all(to_items(key_vectors), "patch", split_axis=0, concat_axis=2, tiled=True)[
                0
            ],
            lax.all_to_all(
                to_items(value_vectors), "patch", split_axis=0, concat_axis=2, tiled=True
            )[0],
            lax.all_to_all(to_items(grad_output), "patch", split_axis=0, concat_axis=2, tiled=True)[
                0
            ],
        ),
    )
    swapped = tuple((result[None] for result in results))
    returned = (
        lax.all_to_all(swapped[0], "patch", split_axis=2, concat_axis=0, tiled=True),
        lax.all_to_all(swapped[1], "patch", split_axis=2, concat_axis=0, tiled=True),
        lax.all_to_all(swapped[2], "patch", split_axis=2, concat_axis=0, tiled=True),
        lax.all_to_all(swapped[3], "patch", split_axis=2, concat_axis=0, tiled=True),
    )
    spatial_out = [from_items(tensor) for tensor in returned]

    def split_heads(tensor):
        return tensor.reshape(
            tensor.shape[0], tensor.shape[1], tensor.shape[2], temporal_heads, head_size
        )

    def merge_heads(tensor):
        return tensor.reshape(tensor.shape[0], tensor.shape[1], tensor.shape[2], half_width)

    time_queries = queries[..., half_width:]
    time_keys = key_vectors[..., half_width:]
    time_values = value_vectors[..., half_width:]
    time_grads = grad_output[..., half_width:]
    position = lax.axis_index("tm")
    first_frame = position * frames_dev
    reach = (WINDOW + frames_dev - 2) // frames_dev
    frame_counts = {}
    for distance in range(1, reach + 1):
        frame_counts[distance] = min(frames_dev, WINDOW - 1 - (distance - 1) * frames_dev)
    arrivals = {}
    for distance in range(1, reach + 1):
        frame_count = frame_counts[distance]
        for direction in (1, -1):
            sent_keys = (
                time_keys[:, frames_dev - frame_count :]
                if direction == 1
                else time_keys[:, :frame_count]
            )
            sent_values = (
                time_values[:, frames_dev - frame_count :]
                if direction == 1
                else time_values[:, :frame_count]
            )
            arrivals[distance, direction] = from_behind(
                (sent_keys, sent_values), "tm", direction * distance
            )
    lower_order = list(range(reach, 0, -1))
    upper_order = list(range(1, reach + 1))
    key_ext = jnp.concatenate(
        [arrivals[distance, 1][0] for distance in lower_order]
        + [time_keys]
        + [arrivals[distance, -1][0] for distance in upper_order],
        axis=1,
    )
    value_ext = jnp.concatenate(
        [arrivals[distance, 1][1] for distance in lower_order]
        + [time_values]
        + [arrivals[distance, -1][1] for distance in upper_order],
        axis=1,
    )
    ext_frames = first_frame - (WINDOW - 1) + jnp.arange(key_ext.shape[1], dtype=jnp.int32)
    starts = lax.dynamic_slice_in_dim(window_start, first_frame, frames_dev)
    allowed_near = window_mask(ext_frames, starts)
    attended_t, grad_q_t, grad_k_ext, grad_v_ext = attention_core(
        split_heads(time_queries),
        split_heads(key_ext),
        split_heads(value_ext),
        split_heads(time_grads),
        allowed_near,
    )
    grad_k_ext = merge_heads(grad_k_ext)
    grad_v_ext = merge_heads(grad_v_ext)
    offsets = {}
    running = 0
    for distance in lower_order:
        offsets[distance, 1] = running
        running = running + frame_counts[distance]
    running = WINDOW - 1 + frames_dev
    for distance in upper_order:
        offsets[distance, -1] = running
        running = running + frame_counts[distance]
    total_keys = grad_k_ext[:, WINDOW - 1 : WINDOW - 1 + frames_dev]
    total_values = grad_v_ext[:, WINDOW - 1 : WINDOW - 1 + frames_dev]
    for distance in range(1, reach + 1):
        frame_count = frame_counts[distance]
        for direction in (1, -1):
            start_at = offsets[distance, direction]
            piece_keys = grad_k_ext[:, start_at : start_at + frame_count]
            piece_values = grad_v_ext[:, start_at : start_at + frame_count]
            back_keys, back_values = (
                from_behind(piece_keys.astype(jnp.bfloat16), "tm", -direction * distance).astype(
                    piece_keys.dtype
                ),
                from_behind(piece_values.astype(jnp.bfloat16), "tm", -direction * distance).astype(
                    piece_values.dtype
                ),
            )
            before = frames_dev - frame_count if direction == 1 else 0
            after = 0 if direction == 1 else frames_dev - frame_count
            padding = ((0, 0), (before, after), (0, 0), (0, 0))
            total_keys = total_keys + jnp.pad(back_keys, padding)
            total_values = total_values + jnp.pad(back_values, padding)
    temporal_out = (
        merge_heads(attended_t),
        merge_heads(grad_q_t).astype(jnp.bfloat16),
        total_keys.astype(jnp.bfloat16),
        total_values.astype(jnp.bfloat16),
    )
    joined = [
        jnp.concatenate([spatial_out[index], temporal_out[index]], axis=-1) for index in range(4)
    ]
    return (joined[0], joined[1], joined[2], joined[3])


def solution(mesh):
    in_specs = (
        P(None, "tm", "patch", None),
        P(None, "tm", "patch", None),
        P(None, "tm", "patch", None),
        P(None, "tm", "patch", None),
        P(),
    )
    out_specs = (
        P(None, "tm", "patch", None),
        P(None, "tm", "patch", None),
        P(None, "tm", "patch", None),
        P(None, "tm", "patch", None),
    )
    return jax.shard_map(
        on_device, mesh=mesh, in_specs=in_specs, out_specs=out_specs, check_vma=False
    )
```

profile of v0, /device:TPU:1, one launch (start us, length us, event | category | flops | bytes accessed | tf_op | source)
XLA Modules:
  0.0 377.4 jit_solution(9611409386311069532)
XLA Ops:
  5.0 7.4 %collective-permute-start.1 = (bf16[1,4,64,512]{3,2,1,0:T(8,128)(2,1)}, bf16[1,4,64,512]{3,2,1,0:T(8,128)(2,1)}, u32[]{:S(2)}, u32[]{:S(2)}) collective-permute-start(bf16[1,4,64,512]{3,2,1,0:T(8,128)(2,1)} %slice.114), channel_id=1, source_target_pairs={{0,48},{16,64},{32,80},{48,96},{64,112},{80,128},{96,144},{112,160... | collective-permute-start | bytes 786440 | tf_op jit(solution)/shard_map/ppermute | solution.py:13
  23.9 10.6 %all-to-all-start = ((bf16[16,1,64,128]{3,2,1,0:T(8,128)(2,1)}), bf16[16,1,64,128]{3,2,1,0:T(8,128)(2,1)S(1)}, u32[]{:S(2)}, u32[]{:S(2)}) async-start(bf16[16,1,64,128]{3,2,1,0:T(8,128)(2,1)} %bitcast.1), calls=%async_computation | async-start | bytes 524288 | tf_op jit(solution)/shard_map/all_to_all | solution.py:90
  41.7 6.5 %collective-permute-start.3 = (bf16[1,4,64,512]{3,2,1,0:T(8,128)(2,1)}, bf16[1,4,64,512]{3,2,1,0:T(8,128)(2,1)S(1)}, u32[]{:S(2)}, u32[]{:S(2)}) collective-permute-start(bf16[1,4,64,512]{3,2,1,0:T(8,128)(2,1)} %slice.114), channel_id=1, source_target_pairs={{0,16},{16,32},{32,48},{48,64},{64,80},{80,96},{96,112},{112,128},... | collective-permute-start | bytes 786440 | tf_op jit(solution)/shard_map/ppermute | solution.py:13
  59.0 7.2 %collective-permute-start.11 = (bf16[1,4,64,512]{3,2,1,0:T(8,128)(2,1)}, bf16[1,4,64,512]{3,2,1,0:T(8,128)(2,1)S(1)}, u32[]{:S(2)}, u32[]{:S(2)}) collective-permute-start(bf16[1,4,64,512]{3,2,1,0:T(8,128)(2,1)} %slice.117), channel_id=1, source_target_pairs={{0,16},{16,32},{32,48},{48,64},{64,80},{80,96},{96,112},{112,128},... | collective-permute-start | bytes 786440 | tf_op jit(solution)/shard_map/ppermute | solution.py:13
  75.0 5.6 %collective-permute-done.12 = bf16[1,4,64,512]{3,2,1,0:T(8,128)(2,1)S(1)} collective-permute-done((bf16[1,4,64,512]{3,2,1,0:T(8,128)(2,1)S(1)}, bf16[1,4,64,512]{3,2,1,0:T(8,128)(2,1)S(1)}, u32[]{:S(2)}, u32[]{:S(2)}) %collective-permute-start.12) | collective-permute-done | bytes 262176 | tf_op jit(solution)/shard_map/ppermute | solution.py:13
  85.4 5.8 %collective-permute-done.15 = bf16[1,3,64,512]{3,2,1,0:T(8,128)(2,1)S(1)} collective-permute-done((bf16[1,3,64,512]{3,2,1,0:T(8,128)(2,1)}, bf16[1,3,64,512]{3,2,1,0:T(8,128)(2,1)S(1)}, u32[]{:S(2)}, u32[]{:S(2)}) %collective-permute-start.15) | collective-permute-done | bytes 196640 | tf_op jit(solution)/shard_map/ppermute | solution.py:13
  99.9 6.7 %reshape.304 = bf16[34,64,8,64]{3,2,1,0:T(8,128)(2,1)} reshape(bf16[1,34,64,512]{3,2,1,0:T(8,128)(2,1)} %constant_dynamic-update-slice_fusion) | data formatting | bytes 4456448 | tf_op jit(solution)/shard_map/reshape.77
  106.6 6.2 %fusion.86 = (f32[64,8,4]{2,1,0:T(8,128)S(1)}, f32[64,8,4,34]{3,2,1,0:T(4,128)S(1)}) fusion(bf16[34,64,8,64]{3,2,1,0:T(8,128)(2,1)} %reshape.305, pred[4,34]{1,0:T(4,128)(4,1)S(1)} %compare_and_fusion, bf16[4,64,8,64]{3,2,1,0:T(8,128)(2,1)S(1)} %copy-done.4), kind=kOutput, calls=%fused_computation.112 | convolution fusion | flops 9191457 | bytes 2777224 | tf_op jit(solution)/shard_map/sub | solution.py:25
  112.8 6.0 %multiply_reduce_fusion.2 = (f32[64,8,4]{2,1,0:T(8,128)S(1)}, f32[64,8,4,34]{3,2,1,0:T(4,128)S(1)}) fusion(f32[64,8,4,34]{3,2,1,0:T(4,128)S(1)} %get-tuple-element.62, f32[64,8,4]{2,1,0:T(8,128)S(1)} %get-tuple-element.61, bf16[4,64,8,64]{3,2,1,0:T(8,128)(2,1)S(1)} %copy-done.5, bf16[34,64,8,64]{3,2,1,0:T(8,128)(2,1)} %reshape.304), kind=kOutput, calls=%fused_computation.41 | convolution fusion | flops 9119744 | bytes 3063808 | tf_op jit(solution)/shard_map/bqphd,bkphd->bphqk/dot_general | solution.py:31
  124.1 9.6 %all-to-all-start.4 = ((bf16[16,1,64,128]{3,2,1,0:T(8,128)(2,1)}), bf16[16,1,64,128]{3,2,1,0:T(8,128)(2,1)}, u32[]{:S(2)}, u32[]{:S(2)}) async-start(bf16[16,1,64,128]{3,2,1,0:T(8,128)(2,1)} %bitcast.178), calls=%async_computation.4 | async-start | bytes 524288 | tf_op jit(solution)/shard_map/all_to_all | solution.py:97
  156.8 8.4 %reshape.319 = f32[1,34,64,512]{3,2,1,0:T(8,128)} reshape(f32[1,34,64,8,64]{4,3,2,1,0:T(8,128)} %copy.104) | data formatting | bytes 8912896 | tf_op jit(solution)/shard_map/reshape | solution.py:117
  167.7 9.2 %all-to-all-start.2 = ((bf16[16,1,64,128]{3,2,1,0:T(8,128)(2,1)}), bf16[16,1,64,128]{3,2,1,0:T(8,128)(2,1)}, u32[]{:S(2)}, u32[]{:S(2)}) async-start(bf16[16,1,64,128]{3,2,1,0:T(8,128)(2,1)} %bitcast.180), calls=%async_computation.2 | async-start | bytes 524288 | tf_op jit(solution)/shard_map/all_to_all | solution.py:94
  184.9 8.5 %collective-permute-start.24 = (bf16[1,4,64,512]{3,2,1,0:T(8,128)(2,1)}, bf16[1,4,64,512]{3,2,1,0:T(8,128)(2,1)}, u32[]{:S(2)}, u32[]{:S(2)}) collective-permute-start(bf16[1,4,64,512]{3,2,1,0:T(8,128)(2,1)} %get-tuple-element.26), channel_id=1, source_target_pairs={{16,0},{32,16},{48,32},{64,48},{80,64},{96,80},{112,96},{128,112},... | collective-permute-start | bytes 786440 | tf_op jit(solution)/shard_map/ppermute | solution.py:13
  195.4 9.8 %all-to-all-start.1 = ((bf16[16,1,64,128]{3,2,1,0:T(8,128)(2,1)}), bf16[16,1,64,128]{3,2,1,0:T(8,128)(2,1)}, u32[]{:S(2)}, u32[]{:S(2)}) async-start(bf16[16,1,64,128]{3,2,1,0:T(8,128)(2,1)} %bitcast.179), calls=%async_computation.1 | async-start | bytes 524288 | tf_op jit(solution)/shard_map/all_to_all | solution.py:91
  213.3 8.4 %reshape.316 = f32[1,34,64,512]{3,2,1,0:T(8,128)} reshape(f32[1,34,64,8,64]{4,3,2,1,0:T(8,128)} %copy.99) | data formatting | bytes 8912896 | tf_op jit(solution)/shard_map/reshape | solution.py:117
  237.3 5.5 %fusion.47 = bf16[2,1024,64]{1,2,0:T(8,128)(2,1)} fusion(bf16[1024,2,64]{0,2,1:T(8,128)(2,1)S(1)} %copy.112, f32[2,1024,1024]{1,2,0:T(8,128)} %get-tuple-element.64, f32[2,1024]{1,0:T(2,128)S(1)} %get-tuple-element.63), kind=kOutput, calls=%fused_computation.36 | convolution fusion | flops 272760832 | bytes 8921088 | tf_op jit(solution)/shard_map/while/body/eval_jaxpr/bphqk,bqphd->bkphd/dot_general | solution.py:44
  247.7 9.3 %all-to-all-start.7 = ((bf16[16,2,4096]{2,1,0:T(2,128)(2,1)}), bf16[16,2,4096]{2,1,0:T(2,128)(2,1)S(1)}, u32[]{:S(2)}, u32[]{:S(2)}) async-start(bf16[16,2,4096]{2,1,0:T(2,128)(2,1)} %reshape.330), calls=%async_computation.7 | async-start | bytes 524288 | tf_op jit(solution)/shard_map/all_to_all | solution.py:107
  257.0 8.2 %multiply_reduce_fusion = (f32[2,1024]{1,0:T(2,128)S(1)}, f32[2,1024,1024]{1,2,0:T(8,128)}) fusion(f32[2,1024,1024]{1,2,0:T(8,128)} %get-tuple-element.64, f32[2,1024]{1,0:T(2,128)S(1)} %get-tuple-element.63, bf16[1024,2,64]{0,2,1:T(8,128)(2,1)} %copy-done.15, bf16[1024,2,64]{0,2,1:T(8,128)(2,1)} %copy.111), kind=kOutput, calls=%fused_computation.4 | convolution fusion | flops 274724864 | bytes 17317888 | tf_op jit(solution)/shard_map/while/body/eval_jaxpr/bqphd,bkphd->bphqk/dot_general | solution.py:31
  276.1 9.2 %all-to-all-start.3 = ((bf16[16,2,4096]{2,1,0:T(2,128)(2,1)}), bf16[16,2,4096]{2,1,0:T(2,128)(2,1)}, u32[]{:S(2)}, u32[]{:S(2)}) async-start(bf16[16,2,4096]{2,1,0:T(2,128)(2,1)} %reshape.324), calls=%async_computation.3 | async-start | bytes 524288 | tf_op jit(solution)/shard_map/all_to_all | solution.py:104
  285.3 7.0 %multiply_convert_fusion = bf16[2,1024,1024]{1,2,0:T(8,128)(2,1)S(1)} fusion(f32[2,1024,1024]{1,2,0:T(8,128)} %get-tuple-element.68, f32[2,1024]{1,0:T(2,128)S(1)} %get-tuple-element.67, f32[2,1024,1024]{1,2,0:T(8,128)} %get-tuple-element.64, f32[2,1024]{1,0:T(2,128)S(1)} %get-tuple-element.63), kind=kLoop, calls=%fused_computation.3 | loop fusion | flops 8388608 | bytes 20987904 | tf_op jit(solution)/shard_map/while/body/eval_jaxpr/convert_element_type | solution.py:35
  303.7 9.0 %all-to-all-start.6 = ((bf16[16,2,4096]{2,1,0:T(2,128)(2,1)}), bf16[16,2,4096]{2,1,0:T(2,128)(2,1)S(1)}, u32[]{:S(2)}, u32[]{:S(2)}) async-start(bf16[16,2,4096]{2,1,0:T(2,128)(2,1)} %reshape.328), calls=%async_computation.6 | async-start | bytes 524288 | tf_op jit(solution)/shard_map/all_to_all | solution.py:106
  315.1 6.5 %collective-permute-start.27 = (bf16[1,4,64,512]{3,2,1,0:T(8,128)(2,1)}, bf16[1,4,64,512]{3,2,1,0:T(8,128)(2,1)}, u32[]{:S(2)}, u32[]{:S(2)}) collective-permute-start(bf16[1,4,64,512]{3,2,1,0:T(8,128)(2,1)} %get-tuple-element.38), channel_id=1, source_target_pairs={{0,32},{16,48},{32,64},{48,80},{64,96},{80,112},{96,128},{112,144}... | collective-permute-start | bytes 786440 | tf_op jit(solution)/shard_map/ppermute | solution.py:13
  350.3 9.8 %all-to-all-start.5 = ((bf16[16,2,4096]{2,1,0:T(2,128)(2,1)}), bf16[16,2,4096]{2,1,0:T(2,128)(2,1)S(1)}, u32[]{:S(2)}, u32[]{:S(2)}) async-start(bf16[16,2,4096]{2,1,0:T(2,128)(2,1)} %reshape.326), calls=%async_computation.5 | async-start | bytes 524288 | tf_op jit(solution)/shard_map/all_to_all | solution.py:105
  366.9 7.2 %all-to-all-done.5 = bf16[16,2,4096]{2,1,0:T(2,128)(2,1)S(1)} async-done(((bf16[16,2,4096]{2,1,0:T(2,128)(2,1)}), bf16[16,2,4096]{2,1,0:T(2,128)(2,1)S(1)}, u32[]{:S(2)}, u32[]{:S(2)}) %all-to-all-start.5) | async-done | bytes 262176 | tf_op jit(solution)/shard_map/all_to_all | solution.py:105
  (202 shorter events, 188.1 us)
Async XLA Ops:
  2.4 95.1 %collective-permute-start.6 = (bf16[1,4,64,512]{3,2,1,0:T(8,128)(2,1)}, bf16[1,4,64,512]{3,2,1,0:T(8,128)(2,1)}, u32[]{:S(2)}, u32[]{:S(2)}) collective-permute-start(bf16[1,4,64,512]{3,2,1,0:T(8,128)(2,1)} %slice.114), channel_id=1, source_target_pairs={{48,0},{64,16},{80,32},{96,48},{112,64},{128,80},{144,96},{160,112... | collective-permute-start | bytes 786440 | tf_op jit(solution)/shard_map/ppermute | solution.py:13
  3.7 92.1 %collective-permute-start.5 = (bf16[1,4,64,512]{3,2,1,0:T(8,128)(2,1)}, bf16[1,4,64,512]{3,2,1,0:T(8,128)(2,1)}, u32[]{:S(2)}, u32[]{:S(2)}) collective-permute-start(bf16[1,4,64,512]{3,2,1,0:T(8,128)(2,1)} %slice.114), channel_id=1, source_target_pairs={{32,0},{48,16},{64,32},{80,48},{96,64},{112,80},{128,96},{144,112}... | collective-permute-start | bytes 786440 | tf_op jit(solution)/shard_map/ppermute | solution.py:13
  5.0 44.2 %collective-permute-start.1 = (bf16[1,4,64,512]{3,2,1,0:T(8,128)(2,1)}, bf16[1,4,64,512]{3,2,1,0:T(8,128)(2,1)}, u32[]{:S(2)}, u32[]{:S(2)}) collective-permute-start(bf16[1,4,64,512]{3,2,1,0:T(8,128)(2,1)} %slice.114), channel_id=1, source_target_pairs={{0,48},{16,64},{32,80},{48,96},{64,112},{80,128},{96,144},{112,160... | collective-permute-start | bytes 786440 | tf_op jit(solution)/shard_map/ppermute | solution.py:13
  14.1 26.9 %collective-permute-start.8 = (bf16[1,3,64,512]{3,2,1,0:T(8,128)(2,1)S(1)}, bf16[1,3,64,512]{3,2,1,0:T(8,128)(2,1)S(1)}, u32[]{:S(2)}, u32[]{:S(2)}) collective-permute-start(bf16[1,3,64,512]{3,2,1,0:T(8,128)(2,1)S(1)} %get-tuple-element.58), channel_id=1, source_target_pairs={{0,64},{16,80},{32,96},{48,112},{64,128},{80,144},{96,160},{112,17... | collective-permute-start | bytes 589832 | tf_op jit(solution)/shard_map/ppermute | solution.py:13
  23.9 100.2 %all-to-all-start = ((bf16[16,1,64,128]{3,2,1,0:T(8,128)(2,1)}), bf16[16,1,64,128]{3,2,1,0:T(8,128)(2,1)S(1)}, u32[]{:S(2)}, u32[]{:S(2)}) async-start(bf16[16,1,64,128]{3,2,1,0:T(8,128)(2,1)} %bitcast.1), calls=%async_computation | async-start | bytes 524288 | tf_op jit(solution)/shard_map/all_to_all | solution.py:90
  53.8 30.1 %collective-permute-start.14 = (bf16[1,4,64,512]{3,2,1,0:T(8,128)(2,1)}, bf16[1,4,64,512]{3,2,1,0:T(8,128)(2,1)S(1)}, u32[]{:S(2)}, u32[]{:S(2)}) collective-permute-start(bf16[1,4,64,512]{3,2,1,0:T(8,128)(2,1)} %slice.117), channel_id=1, source_target_pairs={{48,0},{64,16},{80,32},{96,48},{112,64},{128,80},{144,96},{160,112... | collective-permute-start | bytes 786440 | tf_op jit(solution)/shard_map/ppermute | solution.py:13
  55.1 27.5 %collective-permute-start.13 = (bf16[1,4,64,512]{3,2,1,0:T(8,128)(2,1)}, bf16[1,4,64,512]{3,2,1,0:T(8,128)(2,1)S(1)}, u32[]{:S(2)}, u32[]{:S(2)}) collective-permute-start(bf16[1,4,64,512]{3,2,1,0:T(8,128)(2,1)} %slice.117), channel_id=1, source_target_pairs={{32,0},{48,16},{64,32},{80,48},{96,64},{112,80},{128,96},{144,112}... | collective-permute-start | bytes 786440 | tf_op jit(solution)/shard_map/ppermute | solution.py:13
  124.1 43.7 %all-to-all-start.4 = ((bf16[16,1,64,128]{3,2,1,0:T(8,128)(2,1)}), bf16[16,1,64,128]{3,2,1,0:T(8,128)(2,1)}, u32[]{:S(2)}, u32[]{:S(2)}) async-start(bf16[16,1,64,128]{3,2,1,0:T(8,128)(2,1)} %bitcast.178), calls=%async_computation.4 | async-start | bytes 524288 | tf_op jit(solution)/shard_map/all_to_all | solution.py:97
  167.7 27.6 %all-to-all-start.2 = ((bf16[16,1,64,128]{3,2,1,0:T(8,128)(2,1)}), bf16[16,1,64,128]{3,2,1,0:T(8,128)(2,1)}, u32[]{:S(2)}, u32[]{:S(2)}) async-start(bf16[16,1,64,128]{3,2,1,0:T(8,128)(2,1)} %bitcast.180), calls=%async_computation.2 | async-start | bytes 524288 | tf_op jit(solution)/shard_map/all_to_all | solution.py:94
  177.8 121.3 %collective-permute-start.30 = (bf16[1,3,64,512]{3,2,1,0:T(8,128)(2,1)}, bf16[1,3,64,512]{3,2,1,0:T(8,128)(2,1)}, u32[]{:S(2)}, u32[]{:S(2)}) collective-permute-start(bf16[1,3,64,512]{3,2,1,0:T(8,128)(2,1)} %get-tuple-element.24), channel_id=1, source_target_pairs={{64,0},{80,16},{96,32},{112,48},{128,64},{144,80},{160,96},{176,11... | collective-permute-start | bytes 589832 | tf_op jit(solution)/shard_map/ppermute | solution.py:13
  179.0 134.6 %collective-permute-start.31 = (bf16[1,3,64,512]{3,2,1,0:T(8,128)(2,1)}, bf16[1,3,64,512]{3,2,1,0:T(8,128)(2,1)}, u32[]{:S(2)}, u32[]{:S(2)}) collective-permute-start(bf16[1,3,64,512]{3,2,1,0:T(8,128)(2,1)} %get-tuple-element.25), channel_id=1, source_target_pairs={{0,64},{16,80},{32,96},{48,112},{64,128},{80,144},{96,160},{112,17... | collective-permute-start | bytes 589832 | tf_op jit(solution)/shard_map/ppermute | solution.py:13
  184.9 138.0 %collective-permute-start.24 = (bf16[1,4,64,512]{3,2,1,0:T(8,128)(2,1)}, bf16[1,4,64,512]{3,2,1,0:T(8,128)(2,1)}, u32[]{:S(2)}, u32[]{:S(2)}) collective-permute-start(bf16[1,4,64,512]{3,2,1,0:T(8,128)(2,1)} %get-tuple-element.26), channel_id=1, source_target_pairs={{16,0},{32,16},{48,32},{64,48},{80,64},{96,80},{112,96},{128,112},... | collective-permute-start | bytes 786440 | tf_op jit(solution)/shard_map/ppermute | solution.py:13
  193.4 133.3 %collective-permute-start.29 = (bf16[1,4,64,512]{3,2,1,0:T(8,128)(2,1)}, bf16[1,4,64,512]{3,2,1,0:T(8,128)(2,1)}, u32[]{:S(2)}, u32[]{:S(2)}) collective-permute-start(bf16[1,4,64,512]{3,2,1,0:T(8,128)(2,1)} %get-tuple-element.36), channel_id=1, source_target_pairs={{0,48},{16,64},{32,80},{48,96},{64,112},{80,128},{96,144},{112,160... | collective-permute-start | bytes 786440 | tf_op jit(solution)/shard_map/ppermute | solution.py:13
  195.4 35.5 %all-to-all-start.1 = ((bf16[16,1,64,128]{3,2,1,0:T(8,128)(2,1)}), bf16[16,1,64,128]{3,2,1,0:T(8,128)(2,1)}, u32[]{:S(2)}, u32[]{:S(2)}) async-start(bf16[16,1,64,128]{3,2,1,0:T(8,128)(2,1)} %bitcast.179), calls=%async_computation.1 | async-start | bytes 524288 | tf_op jit(solution)/shard_map/all_to_all | solution.py:91
  225.0 90.1 %collective-permute-start.22 = (bf16[1,3,64,512]{3,2,1,0:T(8,128)(2,1)}, bf16[1,3,64,512]{3,2,1,0:T(8,128)(2,1)}, u32[]{:S(2)}, u32[]{:S(2)}) collective-permute-start(bf16[1,3,64,512]{3,2,1,0:T(8,128)(2,1)} %get-tuple-element.41), channel_id=1, source_target_pairs={{64,0},{80,16},{96,32},{112,48},{128,64},{144,80},{160,96},{176,11... | collective-permute-start | bytes 589832 | tf_op jit(solution)/shard_map/ppermute | solution.py:13
  247.7 28.4 %all-to-all-start.7 = ((bf16[16,2,4096]{2,1,0:T(2,128)(2,1)}), bf16[16,2,4096]{2,1,0:T(2,128)(2,1)S(1)}, u32[]{:S(2)}, u32[]{:S(2)}) async-start(bf16[16,2,4096]{2,1,0:T(2,128)(2,1)} %reshape.330), calls=%async_computation.7 | async-start | bytes 524288 | tf_op jit(solution)/shard_map/all_to_all | solution.py:107
  276.1 27.7 %all-to-all-start.3 = ((bf16[16,2,4096]{2,1,0:T(2,128)(2,1)}), bf16[16,2,4096]{2,1,0:T(2,128)(2,1)}, u32[]{:S(2)}, u32[]{:S(2)}) async-start(bf16[16,2,4096]{2,1,0:T(2,128)(2,1)} %reshape.324), calls=%async_computation.3 | async-start | bytes 524288 | tf_op jit(solution)/shard_map/all_to_all | solution.py:104
  299.1 22.5 %collective-permute-start.23 = (bf16[1,3,64,512]{3,2,1,0:T(8,128)(2,1)}, bf16[1,3,64,512]{3,2,1,0:T(8,128)(2,1)}, u32[]{:S(2)}, u32[]{:S(2)}) collective-permute-start(bf16[1,3,64,512]{3,2,1,0:T(8,128)(2,1)} %get-tuple-element.42), channel_id=1, source_target_pairs={{0,64},{16,80},{32,96},{48,112},{64,128},{80,144},{96,160},{112,17... | collective-permute-start | bytes 589832 | tf_op jit(solution)/shard_map/ppermute | solution.py:13
  303.7 46.6 %all-to-all-start.6 = ((bf16[16,2,4096]{2,1,0:T(2,128)(2,1)}), bf16[16,2,4096]{2,1,0:T(2,128)(2,1)S(1)}, u32[]{:S(2)}, u32[]{:S(2)}) async-start(bf16[16,2,4096]{2,1,0:T(2,128)(2,1)} %reshape.328), calls=%async_computation.6 | async-start | bytes 524288 | tf_op jit(solution)/shard_map/all_to_all | solution.py:106
  315.1 24.0 %collective-permute-start.27 = (bf16[1,4,64,512]{3,2,1,0:T(8,128)(2,1)}, bf16[1,4,64,512]{3,2,1,0:T(8,128)(2,1)}, u32[]{:S(2)}, u32[]{:S(2)}) collective-permute-start(bf16[1,4,64,512]{3,2,1,0:T(8,128)(2,1)} %get-tuple-element.38), channel_id=1, source_target_pairs={{0,32},{16,48},{32,64},{48,80},{64,96},{80,112},{96,128},{112,144}... | collective-permute-start | bytes 786440 | tf_op jit(solution)/shard_map/ppermute | solution.py:13
  322.9 21.9 %collective-permute-start.25 = (bf16[1,4,64,512]{3,2,1,0:T(8,128)(2,1)}, bf16[1,4,64,512]{3,2,1,0:T(8,128)(2,1)}, u32[]{:S(2)}, u32[]{:S(2)}) collective-permute-start(bf16[1,4,64,512]{3,2,1,0:T(8,128)(2,1)} %get-tuple-element.40), channel_id=1, source_target_pairs={{0,16},{16,32},{32,48},{48,64},{64,80},{80,96},{96,112},{112,128},... | collective-permute-start | bytes 786440 | tf_op jit(solution)/shard_map/ppermute | solution.py:13
  335.1 26.9 %collective-permute-start.21 = (bf16[1,4,64,512]{3,2,1,0:T(8,128)(2,1)S(1)}, bf16[1,4,64,512]{3,2,1,0:T(8,128)(2,1)S(1)}, u32[]{:S(2)}, u32[]{:S(2)}) collective-permute-start(bf16[1,4,64,512]{3,2,1,0:T(8,128)(2,1)S(1)} %copy-done.14), channel_id=1, source_target_pairs={{0,48},{16,64},{32,80},{48,96},{64,112},{80,128},{96,144},{112,160... | collective-permute-start | bytes 786440 | tf_op jit(solution)/shard_map/ppermute | solution.py:13
  339.2 22.9 %collective-permute-start.20 = (bf16[1,4,64,512]{3,2,1,0:T(8,128)(2,1)S(1)}, bf16[1,4,64,512]{3,2,1,0:T(8,128)(2,1)S(1)}, u32[]{:S(2)}, u32[]{:S(2)}) collective-permute-start(bf16[1,4,64,512]{3,2,1,0:T(8,128)(2,1)S(1)} %copy-done.13), channel_id=1, source_target_pairs={{48,0},{64,16},{80,32},{96,48},{112,64},{128,80},{144,96},{160,112... | collective-permute-start | bytes 786440 | tf_op jit(solution)/shard_map/ppermute | solution.py:13
  350.3 23.7 %all-to-all-start.5 = ((bf16[16,2,4096]{2,1,0:T(2,128)(2,1)}), bf16[16,2,4096]{2,1,0:T(2,128)(2,1)S(1)}, u32[]{:S(2)}, u32[]{:S(2)}) async-start(bf16[16,2,4096]{2,1,0:T(2,128)(2,1)} %reshape.326), calls=%async_computation.5 | async-start | bytes 524288 | tf_op jit(solution)/shard_map/all_to_all | solution.py:105
  (38 other events, 607.6 us)
where the time goes:
time: 383 us; the launch traced here: 377 us
  starting transfers between devices  174 us (45%)
  local copies, waits for them, and re-layouts  88.9 us (23%)
  matrix products  56.5 us (15%)
  other arithmetic  29.6 us (8%)
  waiting for transfers between devices  26.5 us (7%)
    ppermute x32, starting transfers between devices, from_behind(): return lax.ppermute(array, axis, pairs)  97.5 us
    unnamed x75, local copies, waits for them, and re-layouts  19.4 us
    ppermute x32, waiting for transfers between devices, from_behind(): return lax.ppermute(array, axis, pairs)  19.4 us
    reshape x3, local copies, waits for them, and re-layouts, merge_heads(): tensor.reshape(tensor.shape[0], tensor.shape[1], tensor.shape[2], half_wi...  18.8 us
    another operation x12, local copies, waits for them, and re-layouts  18.7 us
    dot_general x2, matrix products, attention_core(): jnp.einsum('bqphd,bkphd->bphqk', grad_rows, value_rows, preferred_element...  14.2 us
    sub x2, matrix products, attention_core(): exponent = jnp.exp(scores - highest)  11.1 us
    all_to_all x1, starting transfers between devices, on_device(): lax.all_to_all(to_items(queries), 'patch', split_axis=0, concat_axis=2, t...  10.6 us
  transfers between devices with their start and end apart: 40, of which 5 were waited for; matrix products, arithmetic and copies ran while one was open for 44% of the time, Pallas kernels for 0%

commit v1 on v0

v1 whole, which is shorter than its diff:
```python
import functools

import jax
import jax.numpy as jnp
from jax import lax
from jax.experimental import pallas as pl
from jax.experimental.pallas import tpu as pltpu
from jax.sharding import PartitionSpec as P

MESH = pl.DeviceIdType.MESH
BF16 = jnp.bfloat16
F32 = jnp.float32
N = 16
FR = 4
PT = 64
WINDOW = 16
SCALE = 0.125
QB = 256


def dot(a, b, ca, cb):
    return lax.dot_general(a, b, (((ca,), (cb,)), ((), ())), preferred_element_type=F32)


def kernel(
    q_hbm, k_hbm, v_hbm, g_hbm, ws_ref,
    o_ref, dq_ref, dk_ref, dv_ref,
    inp, s_send, t_send, s_in, t_in, t_f32, tr_a, acc, s_out, s_back, t_back,
    in_sem, ss_sem, sr_sem, ts_sem, tr_sem, bs_sem, br_sem, us_sem, ur_sem,
):
    me_t = lax.axis_index("tm")
    me_p = lax.axis_index("patch")

    def patch_peer(j):
        z = (me_p // 2 + j // 2) % 8
        y = (me_p % 2 + j % 2) % 2
        return z * 2 + y

    def tm_peer(j):
        return (me_t + j) % N

    def to_patch(d):
        return (me_t, d)

    def to_tm(e):
        return (e, me_p)

    loads = []
    for half in range(2):
        for a, ref in enumerate((q_hbm, k_hbm, v_hbm, g_hbm)):
            cols = pl.ds(half * 512, 512)
            copy = pltpu.make_async_copy(
                ref.at[0, :, :, cols], inp.at[a, :, :, cols], in_sem.at[half, a]
            )
            copy.start()
            loads.append(copy)

    barrier = pltpu.get_barrier_semaphore()

    def greet(j, carry):
        pl.semaphore_signal(barrier, inc=1, device_id=to_patch(patch_peer(j)), device_id_type=MESH)
        pl.semaphore_signal(barrier, inc=1, device_id=to_tm(tm_peer(j)), device_id_type=MESH)
        return carry

    lax.fori_loop(1, N, greet, 0)

    def pack_spatial(d):
        f = d // 4
        cols = pl.ds(pl.multiple_of((d % 4) * 128, 128), 128)
        q, k, v, g = (inp[a, f, :, cols] for a in range(4))
        out = []
        for c in range(2):
            h = slice(c * 64, c * 64 + 64)
            out.append(jnp.concatenate([q[:, h], g[:, h]], axis=1))
            out.append(jnp.concatenate([k[:, h], v[:, h]], axis=1))
        return out

    for copy in loads[:4]:
        copy.wait()

    def fill_spatial(j, carry):
        d = patch_peer(j)
        parts = pack_spatial(d)
        for c in range(2):
            for s in range(2):
                s_send[d, c, s] = parts[2 * c + s]
        return carry

    lax.fori_loop(1, N, fill_spatial, 0)
    parts = pack_spatial(me_p)
    own_rows = pl.ds(pl.multiple_of(me_p * PT, PT), PT)
    for c in range(2):
        for s in range(2):
            s_in[c, s, own_rows, :] = parts[2 * c + s]

    pl.semaphore_wait(barrier, 2 * (N - 1))

    def s_copy(c, d):
        return pltpu.make_async_remote_copy(
            src_ref=s_send.at[d, c],
            dst_ref=s_in.at[c, :, own_rows, :],
            send_sem=ss_sem.at[c, d],
            recv_sem=sr_sem.at[c, me_p],
            device_id=to_patch(d),
            device_id_type=MESH,
        )

    def s_arrival(c, d):
        return pltpu.make_async_remote_copy(
            src_ref=s_send.at[d, c],
            dst_ref=s_in.at[c, :, pl.ds(pl.multiple_of(d * PT, PT), PT), :],
            send_sem=ss_sem.at[c, d],
            recv_sem=sr_sem.at[c, d],
            device_id=to_patch(d),
            device_id_type=MESH,
        )

    def t_copy(e):
        return pltpu.make_async_remote_copy(
            src_ref=t_send.at[0, e],
            dst_ref=t_in.at[me_t],
            send_sem=ts_sem.at[e],
            recv_sem=tr_sem.at[me_t],
            device_id=to_tm(e),
            device_id_type=MESH,
        )

    def t_arrival(e):
        return pltpu.make_async_remote_copy(
            src_ref=t_send.at[0, e],
            dst_ref=t_in.at[e],
            send_sem=ts_sem.at[e],
            recv_sem=tr_sem.at[e],
            device_id=to_tm(e),
            device_id_type=MESH,
        )

    def b_copy(c, d):
        return pltpu.make_async_remote_copy(
            src_ref=s_out.at[c, :, pl.ds(pl.multiple_of(d * PT, PT), PT), :],
            dst_ref=s_back.at[me_p, c],
            send_sem=bs_sem.at[c, d],
            recv_sem=br_sem.at[c, me_p],
            device_id=to_patch(d),
            device_id_type=MESH,
        )

    def b_arrival(c, d):
        return pltpu.make_async_remote_copy(
            src_ref=s_out.at[c, :, pl.ds(pl.multiple_of(d * PT, PT), PT), :],
            dst_ref=s_back.at[d, c],
            send_sem=bs_sem.at[c, d],
            recv_sem=br_sem.at[c, d],
            device_id=to_patch(d),
            device_id_type=MESH,
        )

    def u_copy(e):
        return pltpu.make_async_remote_copy(
            src_ref=t_send.at[1, e],
            dst_ref=t_back.at[me_t],
            send_sem=us_sem.at[e],
            recv_sem=ur_sem.at[me_t],
            device_id=to_tm(e),
            device_id_type=MESH,
        )

    def u_arrival(e):
        return pltpu.make_async_remote_copy(
            src_ref=t_send.at[1, e],
            dst_ref=t_back.at[e],
            send_sem=us_sem.at[e],
            recv_sem=ur_sem.at[e],
            device_id=to_tm(e),
            device_id_type=MESH,
        )

    def each(peer, act):
        def body(j, carry):
            act(peer(j))
            return carry

        lax.fori_loop(1, N, body, 0)

    each(patch_peer, lambda d: s_copy(0, d).start())

    for copy in loads[4:]:
        copy.wait()

    def pack_temporal(e):
        rows = pl.ds(pl.multiple_of((e // 4) * 16, 16), 16)
        cols = pl.ds(pl.multiple_of(512 + (e % 4) * 128, 128), 128)
        return [inp[a, :, rows, cols] for a in range(4)]

    def send_temporal(e):
        parts = pack_temporal(e)
        for a in range(4):
            t_send[0, e, a] = parts[a]
        t_copy(e).start()

    each(tm_peer, send_temporal)
    each(patch_peer, lambda d: s_copy(1, d).start())
    parts = pack_temporal(me_t)
    for a in range(4):
        t_in[me_t, a] = parts[a]

    def spatial(c):
        each(patch_peer, lambda d: s_arrival(c, d).wait_recv())
        low = lax.broadcasted_iota(jnp.int32, (QB, 128), 1) < 64

        def turn(i, carry):
            rows = pl.ds(pl.multiple_of(i * QB, QB), QB)
            a = s_in[c, 0, rows, :].astype(F32)
            tr_a[:, rows] = jnp.where(low, a * SCALE, a).T.astype(BF16)
            return carry

        lax.fori_loop(0, 1024 // QB, turn, 0)
        acc[...] = jnp.zeros_like(acc)

        def block(i, carry):
            rows = pl.ds(pl.multiple_of(i * QB, QB), QB)
            a = s_in[c, 0, rows, :]
            b = s_in[c, 1]
            zero = jnp.zeros_like(a)
            a_q = jnp.where(low, a * SCALE, zero)
            a_g = jnp.where(low, zero, a)
            scores = dot(a_q, b, 1, 1)
            weight_grad = dot(a_g, b, 1, 1)
            e = jnp.exp(scores - jnp.max(scores, axis=1, keepdims=True))
            w = e * (1.0 / jnp.sum(e, axis=1, keepdims=True))
            delta = jnp.sum(w * weight_grad, axis=1, keepdims=True)
            ds_b = (w * (weight_grad - delta)).astype(BF16)
            w_b = w.astype(BF16)
            out = jnp.where(low, dot(ds_b, b, 1, 0) * SCALE, dot(w_b, b, 1, 0))
            s_out[c, 0, rows, :] = out.astype(BF16)
            acc[0:64, :] += dot(tr_a[0:64, rows], ds_b, 1, 0)
            acc[64:128, :] += dot(tr_a[64:128, rows], w_b, 1, 0)
            return carry

        lax.fori_loop(0, 1024 // QB, block, 0)

        def back(i, carry):
            rows = pl.ds(pl.multiple_of(i * QB, QB), QB)
            s_out[c, 1, rows, :] = acc[:, rows].T.astype(BF16)
            return carry

        lax.fori_loop(0, 1024 // QB, back, 0)
        each(patch_peer, lambda d: b_copy(c, d).start())
        for s in range(2):
            s_back[me_p, c, s] = s_out[c, s, own_rows, :]

    def temporal():
        each(tm_peer, lambda e: t_arrival(e).wait_recv())

        def widen(e, carry):
            for a in range(4):
                rows = pl.ds(pl.multiple_of(e * 64, 64), 64)
                t_f32[a, rows, :] = t_in[e, a].reshape(64, 128).astype(F32)
            return carry

        lax.fori_loop(0, N, widen, 0)
        i0 = lax.broadcasted_iota(jnp.int32, (64, 64), 0)
        i1 = lax.broadcasted_iota(jnp.int32, (64, 64), 1)
        starts = jnp.sum(
            jnp.where(i0 == i1, jnp.broadcast_to(ws_ref[...].astype(F32), (64, 64)), 0.0),
            axis=1, keepdims=True,
        )
        lanes = lax.broadcasted_iota(jnp.int32, (64, 128), 1)
        low = lanes < 64
        frame = jnp.where(low, lanes, lanes - 64).astype(F32)
        allowed = (frame >= starts) & (frame < starts + WINDOW)
        allowed_0 = allowed & low
        allowed_1 = allowed & ~low

        def halves(x, op, fill, mask_0, mask_1):
            r0 = op(jnp.where(mask_0, x, fill), axis=1, keepdims=True)
            r1 = op(jnp.where(mask_1, x, fill), axis=1, keepdims=True)
            return jnp.where(low, r0, r1)

        def one(p):
            rows = pl.ds(p, 64, stride=16)
            q, k, v, g = (t_f32[a, rows, :] for a in range(4))

            def diagonal(x):
                return jnp.concatenate(
                    [jnp.where(low, x, 0.0), jnp.where(low, 0.0, x)], axis=0
                ).astype(BF16)

            q = (q * SCALE).astype(BF16)
            g = g.astype(BF16)
            k_d = diagonal(k)
            v_d = diagonal(v)
            scores = dot(q, k_d, 1, 1)
            weight_grad = dot(g, v_d, 1, 1)
            highest = halves(scores, jnp.max, -1e30, allowed_0, allowed_1)
            e = jnp.where(allowed, jnp.exp(scores - highest), 0.0)
            w = e * (1.0 / halves(e, jnp.sum, 0.0, low, ~low))
            delta = halves(w * weight_grad, jnp.sum, 0.0, low, ~low)
            ds_b = (w * (weight_grad - delta)).astype(BF16)
            w_b = w.astype(BF16)
            o = dot(w_b, v_d, 1, 0)
            dq = dot(ds_b, k_d, 1, 0) * SCALE
            dk = dot(ds_b, q, 0, 0)
            dv = dot(w_b, g, 0, 0)
            dk = jnp.where(low, dk[:64], dk[64:])
            dv = jnp.where(low, dv[:64], dv[64:])
            for a, x in enumerate((o, dq, dk, dv)):
                t_f32[a, rows, :] = x

        def patches(i, carry):
            for u in range(2):
                one(i * 2 + u)
            return carry

        lax.fori_loop(0, 8, patches, 0)

        def narrow(e):
            rows = pl.ds(pl.multiple_of(e * 64, 64), 64)
            return [t_f32[a, rows, :].astype(BF16).reshape(4, 16, 128) for a in range(4)]

        def send_back(e):
            parts = narrow(e)
            for a in range(4):
                t_send[1, e, a] = parts[a]
            u_copy(e).start()

        each(tm_peer, send_back)
        parts = narrow(me_t)
        for a in range(4):
            t_back[me_t, a] = parts[a]

    spatial(0)
    temporal()
    spatial(1)

    outs = (o_ref, dq_ref, dk_ref, dv_ref)

    def unpack_temporal(e):
        rows = pl.ds(pl.multiple_of((e // 4) * 16, 16), 16)
        cols = pl.ds(pl.multiple_of(512 + (e % 4) * 128, 128), 128)
        for a in range(4):
            outs[a][0, :, rows, cols] = t_back[e, a]

    def take_temporal(e):
        u_arrival(e).wait_recv()
        unpack_temporal(e)

    unpack_temporal(me_t)
    each(tm_peer, take_temporal)

    def unpack_spatial(d):
        f = d // 4
        cols = pl.ds(pl.multiple_of((d % 4) * 128, 128), 128)
        for s, (low_ref, high_ref) in enumerate(((dq_ref, o_ref), (dk_ref, dv_ref))):
            x, y = s_back[d, 0, s], s_back[d, 1, s]
            low_ref[0, f, :, cols] = jnp.concatenate([x[:, :64], y[:, :64]], axis=1)
            high_ref[0, f, :, cols] = jnp.concatenate([x[:, 64:], y[:, 64:]], axis=1)

    unpack_spatial(me_p)
    each(patch_peer, lambda d: b_arrival(0, d).wait_recv())

    def take_spatial(d):
        b_arrival(1, d).wait_recv()
        unpack_spatial(d)

    each(patch_peer, take_spatial)

    def drain_patch(d):
        for c in range(2):
            s_copy(c, d).wait_send()
            b_copy(c, d).wait_send()

    def drain_tm(e):
        t_copy(e).wait_send()
        u_copy(e).wait_send()

    each(patch_peer, drain_patch)
    each(tm_peer, drain_tm)


def on_device(queries, key_vectors, value_vectors, grad_output, window_start):
    anywhere = pl.BlockSpec(memory_space=pltpu.HBM)
    vmem = pl.BlockSpec(memory_space=pltpu.VMEM)
    dma = pltpu.SemaphoreType.DMA
    shape = jax.ShapeDtypeStruct((1, FR, PT, 1024), BF16)
    return pl.pallas_call(
        kernel,
        out_shape=(shape,) * 4,
        in_specs=[anywhere] * 4 + [vmem],
        out_specs=(vmem,) * 4,
        scratch_shapes=[
            pltpu.VMEM((4, FR, PT, 1024), BF16),
            pltpu.VMEM((N, 2, 2, PT, 128), BF16),
            pltpu.VMEM((2, N, 4, FR, 16, 128), BF16),
            pltpu.VMEM((2, 2, 1024, 128), BF16),
            pltpu.VMEM((N, 4, FR, 16, 128), BF16),
            pltpu.VMEM((4, 1024, 128), F32),
            pltpu.VMEM((128, 1024), BF16),
            pltpu.VMEM((128, 1024), F32),
            pltpu.VMEM((2, 2, 1024, 128), BF16),
            pltpu.VMEM((N, 2, 2, PT, 128), BF16),
            pltpu.VMEM((N, 4, FR, 16, 128), BF16),
            dma((2, 4)),
            dma((2, N)), dma((2, N)), dma((N,)), dma((N,)),
            dma((2, N)), dma((2, N)), dma((N,)), dma((N,)),
        ],
        compiler_params=pltpu.CompilerParams(
            collective_id=0, has_side_effects=True, vmem_limit_bytes=60 << 20
        ),
        name="attention",
    )(queries, key_vectors, value_vectors, grad_output, window_start.reshape(1, 64))


def solution(mesh):
    spec = P(None, "tm", "patch", None)
    return jax.shard_map(
        on_device,
        mesh=mesh,
        in_specs=(spec,) * 4 + (P(),),
        out_specs=(spec,) * 4,
        check_vma=False,
    )
```

time: 383 us -> 74.1 us (0.19); the launches traced: 377 us -> 72.6 us
  starting transfers between devices: 174 us -> 0 us
  local copies, waits for them, and re-layouts: 88.9 us -> 5.18 us
  Pallas kernels: 0 us -> 66.8 us
  matrix products: 56.5 us -> 0 us
  other arithmetic: 29.6 us -> 0 us
  waiting for transfers between devices: 26.5 us -> 0 us
    ppermute x32 -> x0, starting transfers between devices: 97.5 us -> none  [from_behind(): return lax.ppermute(array, axis, pairs)]
    all_to_all x8 -> x0, starting transfers between devices: 76.7 us -> none  [the longest x1 10.6 us: on_device(): lax.all_to_all(to_items(queries), 'patch', split_axis=0, concat_axis=2, t...]
    pallas_call x0 -> x1, Pallas kernels: none -> 66.8 us  [on_device(): pl.pallas_call(kernel, out_shape=(shape,) * 4, in_specs=[anywhere] * 4 +...]
    dot_general x10 -> x0, matrix products: 45.4 us -> none  [the longest x2 14.2 us: attention_core(): jnp.einsum('bqphd,bkphd->bphqk', grad_rows, value_rows, preferred_element...]
    reshape x11 -> x0, local copies, waits for them, and re-layouts: 22.1 us -> none  [the longest x3 18.8 us: merge_heads(): tensor.reshape(tensor.shape[0], tensor.shape[1], tensor.shape[2], half_wi...]
    ppermute x32 -> x0, waiting for transfers between devices: 19.4 us -> none  [from_behind(): return lax.ppermute(array, axis, pairs)]
    another operation x12 -> x0, local copies, waits for them, and re-layouts: 18.7 us -> none
    unnamed x75 -> x10, local copies, waits for them, and re-layouts: 19.4 us -> 5.18 us
  transfers between devices with their start and end apart: 40 -> 0, of which waited for: 5 -> 0; matrix products, arithmetic and copies ran while one was open for 44% -> 0% of each run, Pallas kernels for 0% -> 0%
where the time goes in v1:
time: 74.1 us; the launch traced here: 72.6 us
  Pallas kernels  66.8 us (90%)
  local copies, waits for them, and re-layouts  5.18 us (7%)
    pallas_call x1, Pallas kernels, on_device(): pl.pallas_call(kernel, out_shape=(shape,) * 4, in_specs=[anywhere] * 4 +...  66.8 us
    unnamed x10, local copies, waits for them, and re-layouts  5.18 us

profile of v1, /device:TPU:1, one launch (start us, length us, event | category | flops | bytes accessed | tf_op | source)
XLA Modules:
  0.0 72.6 jit_solution(3227061400860121619)
XLA Ops:
  0.6 66.8 %attention.1 = (bf16[1,4,64,1024]{3,2,1,0:T(8,128)(2,1)}, bf16[1,4,64,1024]{3,2,1,0:T(8,128)(2,1)}, bf16[1,4,64,1024]{3,2,1,0:T(8,128)(2,1)}, bf16[1,4,64,1024]{3,2,1,0:T(8,128)(2,1)}) custom-call(bf16[1,4,64,1024]{3,2,1,0:T(8,128)(2,1)} %q_hbm.1, bf16[1,4,64,1024]{3,2,1,0:T(8,128)(2,1)} %k_hbm.1, bf16[1,4,64,1024]{3,2,1,0:T(8,128)(2,1)} %v_hbm.1, ...), custom_call_target="tpu_custom_call" | custom-call | tf_op jit(solution)/shard_map/attention/pallas_call | solution.py:386
  67.4 0.0 copy-start.2
  67.4 1.9 %copy.13 = bf16[1,4,64,1024]{3,2,1,0:T(8,128)(2,1)} copy(bf16[1,4,64,1024]{3,2,1,0:T(8,128)(2,1)} %get-tuple-element.8) | data formatting | bytes 1048576
  69.4 0.0 copy-done.2
  69.4 0.0 copy-start.1
  69.4 0.8 %copy.14 = bf16[1,4,64,1024]{3,2,1,0:T(8,128)(2,1)} copy(bf16[1,4,64,1024]{3,2,1,0:T(8,128)(2,1)S(1)} %copy-done.2) | data formatting | bytes 1048576
  70.2 0.4 copy-done.1
  70.6 0.0 copy-start
  70.6 0.8 %copy.15 = bf16[1,4,64,1024]{3,2,1,0:T(8,128)(2,1)} copy(bf16[1,4,64,1024]{3,2,1,0:T(8,128)(2,1)S(1)} %copy-done.1) | data formatting | bytes 1048576
  71.4 0.4 copy-done
  71.8 0.8 %copy.16 = bf16[1,4,64,1024]{3,2,1,0:T(8,128)(2,1)} copy(bf16[1,4,64,1024]{3,2,1,0:T(8,128)(2,1)S(1)} %copy-done) | data formatting | bytes 1048576
Async XLA Ops:
  67.4 1.9 %copy-start.2 = (bf16[1,4,64,1024]{3,2,1,0:T(8,128)(2,1)S(1)}, bf16[1,4,64,1024]{3,2,1,0:T(8,128)(2,1)}, u32[]{:S(2)}) copy-start(bf16[1,4,64,1024]{3,2,1,0:T(8,128)(2,1)} %get-tuple-element.9) | copy-start | bytes 1572868
  69.4 1.2 %copy-start.1 = (bf16[1,4,64,1024]{3,2,1,0:T(8,128)(2,1)S(1)}, bf16[1,4,64,1024]{3,2,1,0:T(8,128)(2,1)}, u32[]{:S(2)}) copy-start(bf16[1,4,64,1024]{3,2,1,0:T(8,128)(2,1)} %get-tuple-element.10) | copy-start | bytes 1572868
  70.6 1.2 %copy-start = (bf16[1,4,64,1024]{3,2,1,0:T(8,128)(2,1)S(1)}, bf16[1,4,64,1024]{3,2,1,0:T(8,128)(2,1)}, u32[]{:S(2)}) copy-start(bf16[1,4,64,1024]{3,2,1,0:T(8,128)(2,1)} %get-tuple-element.11) | copy-start | bytes 1572868

commit v2 on v1

--- a/solution.py
+++ b/solution.py
@@ -15,6 +15,7 @@
 PT = 64
 WINDOW = 16
 SCALE = 0.125
+GROUP = 4
 QB = 256
 
 
@@ -23,10 +24,10 @@
 
 
 def kernel(
-    q_hbm, k_hbm, v_hbm, g_hbm, ws_ref,
+    q_hbm, k_hbm, v_hbm, g_hbm, ws_hbm,
     o_ref, dq_ref, dk_ref, dv_ref,
-    inp, s_send, t_send, s_in, t_in, t_f32, tr_a, acc, s_out, s_back, t_back,
-    in_sem, ss_sem, sr_sem, ts_sem, tr_sem, bs_sem, br_sem, us_sem, ur_sem,
+    ws_ref, inp, s_send, t_send, s_in, t_in, t_f32, t_res, tr_a, acc, s_out, s_back, t_back,
+    ws_sem, in_sem, ss_sem, sr_sem, ts_sem, tr_sem, bs_sem, br_sem, us_sem, ur_sem,
 ):
     me_t = lax.axis_index("tm")
     me_p = lax.axis_index("patch")
@@ -55,6 +56,9 @@
             copy.start()
             loads.append(copy)
 
+    ws_copy = pltpu.make_async_copy(ws_hbm, ws_ref, ws_sem)
+    ws_copy.start()
+
     barrier = pltpu.get_barrier_semaphore()
 
     def greet(j, carry):
@@ -64,36 +68,17 @@
 
     lax.fori_loop(1, N, greet, 0)
 
-    def pack_spatial(d):
+    def pack_spatial(c, d):
         f = d // 4
         cols = pl.ds(pl.multiple_of((d % 4) * 128, 128), 128)
         q, k, v, g = (inp[a, f, :, cols] for a in range(4))
-        out = []
-        for c in range(2):
-            h = slice(c * 64, c * 64 + 64)
-            out.append(jnp.concatenate([q[:, h], g[:, h]], axis=1))
-            out.append(jnp.concatenate([k[:, h], v[:, h]], axis=1))
-        return out
-
-    for copy in loads[:4]:
-        copy.wait()
-
-    def fill_spatial(j, carry):
-        d = patch_peer(j)
-        parts = pack_spatial(d)
-        for c in range(2):
-            for s in range(2):
-                s_send[d, c, s] = parts[2 * c + s]
-        return carry
-
-    lax.fori_loop(1, N, fill_spatial, 0)
-    parts = pack_spatial(me_p)
+        h = slice(c * 64, c * 64 + 64)
+        return (
+            jnp.concatenate([q[:, h], g[:, h]], axis=1),
+            jnp.concatenate([k[:, h], v[:, h]], axis=1),
+        )
+
     own_rows = pl.ds(pl.multiple_of(me_p * PT, PT), PT)
-    for c in range(2):
-        for s in range(2):
-            s_in[c, s, own_rows, :] = parts[2 * c + s]
-
-    pl.semaphore_wait(barrier, 2 * (N - 1))
 
     def s_copy(c, d):
         return pltpu.make_async_remote_copy(
@@ -182,8 +167,20 @@
 
         lax.fori_loop(1, N, body, 0)
 
-    each(patch_peer, lambda d: s_copy(0, d).start())
-
+    for copy in loads[:4]:
+        copy.wait()
+    pl.semaphore_wait(barrier, 2 * (N - 1))
+
+    def send_spatial(c):
+        def act(d):
+            parts = pack_spatial(c, d)
+            for s in range(2):
+                s_send[d, c, s] = parts[s]
+            s_copy(c, d).start()
+
+        each(patch_peer, act)
+
+    send_spatial(0)
     for copy in loads[4:]:
         copy.wait()
 
@@ -199,7 +196,11 @@
         t_copy(e).start()
 
     each(tm_peer, send_temporal)
-    each(patch_peer, lambda d: s_copy(1, d).start())
+    send_spatial(1)
+    for c in range(2):
+        parts = pack_spatial(c, me_p)
+        for s in range(2):
+            s_in[c, s, own_rows, :] = parts[s]
     parts = pack_temporal(me_t)
     for a in range(4):
         t_in[me_t, a] = parts[a]
@@ -250,6 +251,7 @@
             s_back[me_p, c, s] = s_out[c, s, own_rows, :]
 
     def temporal():
+        ws_copy.wait()
         each(tm_peer, lambda e: t_arrival(e).wait_recv())
 
         def widen(e, carry):
@@ -277,46 +279,45 @@
             r1 = op(jnp.where(mask_1, x, fill), axis=1, keepdims=True)
             return jnp.where(low, r0, r1)
 
-        def one(p):
-            rows = pl.ds(p, 64, stride=16)
-            q, k, v, g = (t_f32[a, rows, :] for a in range(4))
-
-            def diagonal(x):
-                return jnp.concatenate(
-                    [jnp.where(low, x, 0.0), jnp.where(low, 0.0, x)], axis=0
-                ).astype(BF16)
-
-            q = (q * SCALE).astype(BF16)
-            g = g.astype(BF16)
-            k_d = diagonal(k)
-            v_d = diagonal(v)
-            scores = dot(q, k_d, 1, 1)
-            weight_grad = dot(g, v_d, 1, 1)
-            highest = halves(scores, jnp.max, -1e30, allowed_0, allowed_1)
-            e = jnp.where(allowed, jnp.exp(scores - highest), 0.0)
-            w = e * (1.0 / halves(e, jnp.sum, 0.0, low, ~low))
-            delta = halves(w * weight_grad, jnp.sum, 0.0, low, ~low)
-            ds_b = (w * (weight_grad - delta)).astype(BF16)
-            w_b = w.astype(BF16)
-            o = dot(w_b, v_d, 1, 0)
-            dq = dot(ds_b, k_d, 1, 0) * SCALE
-            dk = dot(ds_b, q, 0, 0)
-            dv = dot(w_b, g, 0, 0)
-            dk = jnp.where(low, dk[:64], dk[64:])
-            dv = jnp.where(low, dv[:64], dv[64:])
-            for a, x in enumerate((o, dq, dk, dv)):
-                t_f32[a, rows, :] = x
+        def diagonal(x):
+            return jnp.concatenate(
+                [jnp.where(low, x, 0.0), jnp.where(low, 0.0, x)], axis=0
+            ).astype(BF16)
 
         def patches(i, carry):
-            for u in range(2):
-                one(i * 2 + u)
-            return carry
-
-        lax.fori_loop(0, 8, patches, 0)
+            group = [pl.ds(i * GROUP + u, 64, stride=16) for u in range(GROUP)]
+            items = []
+            for rows in group:
+                q, k, v, g = (t_f32[a, rows, :] for a in range(4))
+                items.append(((q * SCALE).astype(BF16), diagonal(k), diagonal(v), g.astype(BF16)))
+            scores = [dot(q, k_d, 1, 1) for q, k_d, v_d, g in items]
+            weight_grads = [dot(g, v_d, 1, 1) for q, k_d, v_d, g in items]
+            highest = [halves(x, jnp.max, -1e30, allowed_0, allowed_1) for x in scores]
+            exps = [
+                jnp.where(allowed, jnp.exp(x - m), 0.0) for x, m in zip(scores, highest)
+            ]
+            ws = [e * (1.0 / halves(e, jnp.sum, 0.0, low, ~low)) for e in exps]
+            deltas = [
+                halves(w * x, jnp.sum, 0.0, low, ~low) for w, x in zip(ws, weight_grads)
+            ]
+            grads = [
+                (w * (x - m)).astype(BF16) for w, x, m in zip(ws, weight_grads, deltas)
+            ]
+            ws = [w.astype(BF16) for w in ws]
+            for rows, (q, k_d, v_d, g), w_b, ds_b in zip(group, items, ws, grads):
+                dk = dot(ds_b, q, 0, 0)
+                dv = dot(w_b, g, 0, 0)
+                t_res[0, rows, :] = dot(w_b, v_d, 1, 0)
+                t_res[1, rows, :] = dot(ds_b, k_d, 1, 0) * SCALE
+                t_res[2, rows, :] = jnp.where(low, dk[:64], dk[64:])
+                t_res[3, rows, :] = jnp.where(low, dv[:64], dv[64:])
+            return carry
+
+        lax.fori_loop(0, 16 // GROUP, patches, 0)
 
         def narrow(e):
             rows = pl.ds(pl.multiple_of(e * 64, 64), 64)
-            return [t_f32[a, rows, :].astype(BF16).reshape(4, 16, 128) for a in range(4)]
+            return [t_res[a, rows, :].astype(BF16).reshape(4, 16, 128) for a in range(4)]
 
         def send_back(e):
             parts = narrow(e)
@@ -359,16 +360,10 @@
     unpack_spatial(me_p)
     each(patch_peer, lambda d: b_arrival(0, d).wait_recv())
 
-    def take_spatial(d):
-        b_arrival(1, d).wait_recv()
-        unpack_spatial(d)
-
-    each(patch_peer, take_spatial)
-
     def drain_patch(d):
         for c in range(2):
             s_copy(c, d).wait_send()
-            b_copy(c, d).wait_send()
+        b_copy(0, d).wait_send()
 
     def drain_tm(e):
         t_copy(e).wait_send()
@@ -376,6 +371,25 @@
 
     each(patch_peer, drain_patch)
     each(tm_peer, drain_tm)
+
+    def take_spatial(d):
+        b_arrival(1, d).wait_recv()
+        b_copy(1, d).wait_send()
+        unpack_spatial(d)
+
+    each(patch_peer, take_spatial)
+
+
+def emit(*refs):
+    sem = refs[8]
+    copies = [
+        pltpu.make_async_copy(src, dst, sem.at[a])
+        for a, (src, dst) in enumerate(zip(refs[:4], refs[4:8]))
+    ]
+    for copy in copies:
+        copy.start()
+    for copy in copies:
+        copy.wait()
 
 
 def on_device(queries, key_vectors, value_vectors, grad_output, window_start):
@@ -383,32 +397,43 @@
     vmem = pl.BlockSpec(memory_space=pltpu.VMEM)
     dma = pltpu.SemaphoreType.DMA
     shape = jax.ShapeDtypeStruct((1, FR, PT, 1024), BF16)
-    return pl.pallas_call(
+    results = pl.pallas_call(
         kernel,
         out_shape=(shape,) * 4,
-        in_specs=[anywhere] * 4 + [vmem],
+        in_specs=[anywhere] * 5,
         out_specs=(vmem,) * 4,
         scratch_shapes=[
+            pltpu.VMEM((1, 64), jnp.int32),
             pltpu.VMEM((4, FR, PT, 1024), BF16),
             pltpu.VMEM((N, 2, 2, PT, 128), BF16),
             pltpu.VMEM((2, N, 4, FR, 16, 128), BF16),
             pltpu.VMEM((2, 2, 1024, 128), BF16),
             pltpu.VMEM((N, 4, FR, 16, 128), BF16),
             pltpu.VMEM((4, 1024, 128), F32),
+            pltpu.VMEM((4, 1024, 128), F32),
             pltpu.VMEM((128, 1024), BF16),
             pltpu.VMEM((128, 1024), F32),
             pltpu.VMEM((2, 2, 1024, 128), BF16),
             pltpu.VMEM((N, 2, 2, PT, 128), BF16),
             pltpu.VMEM((N, 4, FR, 16, 128), BF16),
-            dma((2, 4)),
+            dma, dma((2, 4)),
             dma((2, N)), dma((2, N)), dma((N,)), dma((N,)),
             dma((2, N)), dma((2, N)), dma((N,)), dma((N,)),
         ],
         compiler_params=pltpu.CompilerParams(
-            collective_id=0, has_side_effects=True, vmem_limit_bytes=60 << 20
+            collective_id=0, has_side_effects=True, vmem_limit_bytes=52900 << 10
         ),
         name="attention",
     )(queries, key_vectors, value_vectors, grad_output, window_start.reshape(1, 64))
+    return pl.pallas_call(
+        emit,
+        out_shape=(shape,) * 4,
+        in_specs=[vmem] * 4,
+        out_specs=(anywhere,) * 4,
+        scratch_shapes=[dma((4,))],
+        compiler_params=pltpu.CompilerParams(vmem_limit_bytes=6 << 20),
+        name="emit",
+    )(*results)
 
 
 def solution(mesh):

time: 74.1 us -> 67 us (0.904); the launches traced: 72.6 us -> 66.9 us
  local copies, waits for them, and re-layouts: 5.18 us -> 0.65 us
  Pallas kernels: 66.8 us -> 65.6 us
    unnamed x10 -> x2, local copies, waits for them, and re-layouts: 5.18 us -> 0.65 us
    pallas_call x1 -> x2, Pallas kernels: 66.8 us -> 65.6 us  [the longest x1 64.2 us: on_device(): pl.pallas_call(kernel, out_shape=(shape,) * 4, in_specs=[anywhere] * 5, o...]
where the time goes in v2:
time: 67 us; the launch traced here: 66.9 us
  Pallas kernels  65.6 us (98%)
    pallas_call x1, Pallas kernels, on_device(): pl.pallas_call(kernel, out_shape=(shape,) * 4, in_specs=[anywhere] * 5, o...  64.2 us
    pallas_call x1, Pallas kernels, on_device(): pl.pallas_call(emit, out_shape=(shape,) * 4, in_specs=[vmem] * 4, out_spe...  1.35 us

profile of v2, /device:TPU:1, one launch (start us, length us, event | category | flops | bytes accessed | tf_op | source)
XLA Modules:
  0.0 66.9 jit_solution(144237560804676332)
XLA Ops:
  0.6 0.0 copy-start
  0.6 0.6 copy-done
  1.3 64.2 %attention.1 = (bf16[1,4,64,1024]{3,2,1,0:T(8,128)(2,1)S(1)}, bf16[1,4,64,1024]{3,2,1,0:T(8,128)(2,1)S(1)}, bf16[1,4,64,1024]{3,2,1,0:T(8,128)(2,1)S(1)}, bf16[1,4,64,1024]{3,2,1,0:T(8,128)(2,1)S(1)}) custom-call(bf16[1,4,64,1024]{3,2,1,0:T(8,128)(2,1)} %q_hbm.1, bf16[1,4,64,1024]{3,2,1,0:T(8,128)(2,1)} %k_hbm.1, bf16[1,4,64,1024]{3,2,1,0:T(8,128)(2,1)} %v_hbm.1, ...), custom_call_target="tpu_custom_call" | custom-call | tf_op jit(solution)/shard_map/attention/pallas_call | solution.py:400
  65.5 1.3 %emit.1 = (bf16[1,4,64,1024]{3,2,1,0:T(8,128)(2,1)}, bf16[1,4,64,1024]{3,2,1,0:T(8,128)(2,1)}, bf16[1,4,64,1024]{3,2,1,0:T(8,128)(2,1)}, bf16[1,4,64,1024]{3,2,1,0:T(8,128)(2,1)}) custom-call(bf16[1,4,64,1024]{3,2,1,0:T(8,128)(2,1)S(1)} %get-tuple-element.8.refs_0_, bf16[1,4,64,1024]{3,2,1,0:T(8,128)(2,1)S(1)} %get-tuple-element.9.refs_1_, ...), custom_call_target="tpu_custom_call" | custom-call | tf_op jit(solution)/shard_map/emit/pallas_call | solution.py:428
Async XLA Ops:
  0.6 0.7 copy-start

commit v3 on v2

--- a/solution.py
+++ b/solution.py
@@ -27,7 +27,7 @@
     q_hbm, k_hbm, v_hbm, g_hbm, ws_hbm,
     o_ref, dq_ref, dk_ref, dv_ref,
     ws_ref, inp, s_send, t_send, s_in, t_in, t_f32, t_res, tr_a, acc, s_out, s_back, t_back,
-    ws_sem, in_sem, ss_sem, sr_sem, ts_sem, tr_sem, bs_sem, br_sem, us_sem, ur_sem,
+    ws_sem, in_sem, ss_sem, sr_sem, ts_sem, tr_sem, bs_sem, b0_sem, br_sem, us_sem, ur_sem,
 ):
     me_t = lax.axis_index("tm")
     me_p = lax.axis_index("patch")
@@ -45,6 +45,15 @@
 
     def to_tm(e):
         return (e, me_p)
+
+    barrier = pltpu.get_barrier_semaphore()
+
+    def greet(j, carry):
+        pl.semaphore_signal(barrier, inc=1, device_id=to_patch(patch_peer(j)), device_id_type=MESH)
+        pl.semaphore_signal(barrier, inc=1, device_id=to_tm(tm_peer(j)), device_id_type=MESH)
+        return carry
+
+    lax.fori_loop(1, N, greet, 0)
 
     loads = []
     for half in range(2):
@@ -59,15 +68,6 @@
     ws_copy = pltpu.make_async_copy(ws_hbm, ws_ref, ws_sem)
     ws_copy.start()
 
-    barrier = pltpu.get_barrier_semaphore()
-
-    def greet(j, carry):
-        pl.semaphore_signal(barrier, inc=1, device_id=to_patch(patch_peer(j)), device_id_type=MESH)
-        pl.semaphore_signal(barrier, inc=1, device_id=to_tm(tm_peer(j)), device_id_type=MESH)
-        return carry
-
-    lax.fori_loop(1, N, greet, 0)
-
     def pack_spatial(c, d):
         f = d // 4
         cols = pl.ds(pl.multiple_of((d % 4) * 128, 128), 128)
@@ -84,19 +84,19 @@
         return pltpu.make_async_remote_copy(
             src_ref=s_send.at[d, c],
             dst_ref=s_in.at[c, :, own_rows, :],
-            send_sem=ss_sem.at[c, d],
-            recv_sem=sr_sem.at[c, me_p],
+            send_sem=ss_sem.at[c],
+            recv_sem=sr_sem.at[c],
             device_id=to_patch(d),
             device_id_type=MESH,
         )
 
-    def s_arrival(c, d):
-        return pltpu.make_async_remote_copy(
-            src_ref=s_send.at[d, c],
-            dst_ref=s_in.at[c, :, pl.ds(pl.multiple_of(d * PT, PT), PT), :],
-            send_sem=ss_sem.at[c, d],
-            recv_sem=sr_sem.at[c, d],
-            device_id=to_patch(d),
+    def s_all(c):
+        return pltpu.make_async_remote_copy(
+            src_ref=s_send.at[pl.ds(0, N - 1), c],
+            dst_ref=s_in.at[c, :, pl.ds(0, (N - 1) * PT), :],
+            send_sem=ss_sem.at[c],
+            recv_sem=sr_sem.at[c],
+            device_id=to_patch(patch_peer(1)),
             device_id_type=MESH,
         )
 
@@ -104,19 +104,19 @@
         return pltpu.make_async_remote_copy(
             src_ref=t_send.at[0, e],
             dst_ref=t_in.at[me_t],
-            send_sem=ts_sem.at[e],
-            recv_sem=tr_sem.at[me_t],
+            send_sem=ts_sem,
+            recv_sem=tr_sem,
             device_id=to_tm(e),
             device_id_type=MESH,
         )
 
-    def t_arrival(e):
-        return pltpu.make_async_remote_copy(
-            src_ref=t_send.at[0, e],
-            dst_ref=t_in.at[e],
-            send_sem=ts_sem.at[e],
-            recv_sem=tr_sem.at[e],
-            device_id=to_tm(e),
+    def t_all():
+        return pltpu.make_async_remote_copy(
+            src_ref=t_send.at[0, pl.ds(0, N - 1)],
+            dst_ref=t_in.at[pl.ds(0, N - 1)],
+            send_sem=ts_sem,
+            recv_sem=tr_sem,
+            device_id=to_tm(tm_peer(1)),
             device_id_type=MESH,
         )
 
@@ -124,19 +124,29 @@
         return pltpu.make_async_remote_copy(
             src_ref=s_out.at[c, :, pl.ds(pl.multiple_of(d * PT, PT), PT), :],
             dst_ref=s_back.at[me_p, c],
-            send_sem=bs_sem.at[c, d],
-            recv_sem=br_sem.at[c, me_p],
+            send_sem=bs_sem.at[c],
+            recv_sem=br_sem.at[me_p] if c else b0_sem,
             device_id=to_patch(d),
             device_id_type=MESH,
         )
 
-    def b_arrival(c, d):
-        return pltpu.make_async_remote_copy(
-            src_ref=s_out.at[c, :, pl.ds(pl.multiple_of(d * PT, PT), PT), :],
-            dst_ref=s_back.at[d, c],
-            send_sem=bs_sem.at[c, d],
-            recv_sem=br_sem.at[c, d],
+    def b_arrival(d):
+        return pltpu.make_async_remote_copy(
+            src_ref=s_out.at[1, :, pl.ds(pl.multiple_of(d * PT, PT), PT), :],
+            dst_ref=s_back.at[d, 1],
+            send_sem=bs_sem.at[1],
+            recv_sem=br_sem.at[d],
             device_id=to_patch(d),
+            device_id_type=MESH,
+        )
+
+    def b_all(c):
+        return pltpu.make_async_remote_copy(
+            src_ref=s_out.at[c, :, pl.ds(0, (N - 1) * PT), :],
+            dst_ref=s_back.at[pl.ds(0, N - 1), c],
+            send_sem=bs_sem.at[c],
+            recv_sem=b0_sem,
+            device_id=to_patch(patch_peer(1)),
             device_id_type=MESH,
         )
 
@@ -144,19 +154,19 @@
         return pltpu.make_async_remote_copy(
             src_ref=t_send.at[1, e],
             dst_ref=t_back.at[me_t],
-            send_sem=us_sem.at[e],
-            recv_sem=ur_sem.at[me_t],
+            send_sem=us_sem,
+            recv_sem=ur_sem,
             device_id=to_tm(e),
             device_id_type=MESH,
         )
 
-    def u_arrival(e):
-        return pltpu.make_async_remote_copy(
-            src_ref=t_send.at[1, e],
-            dst_ref=t_back.at[e],
-            send_sem=us_sem.at[e],
-            recv_sem=ur_sem.at[e],
-            device_id=to_tm(e),
+    def u_all():
+        return pltpu.make_async_remote_copy(
+            src_ref=t_send.at[1, pl.ds(0, N - 1)],
+            dst_ref=t_back.at[pl.ds(0, N - 1)],
+            send_sem=us_sem,
+            recv_sem=ur_sem,
+            device_id=to_tm(tm_peer(1)),
             device_id_type=MESH,
         )
 
@@ -171,16 +181,12 @@
         copy.wait()
     pl.semaphore_wait(barrier, 2 * (N - 1))
 
-    def send_spatial(c):
-        def act(d):
-            parts = pack_spatial(c, d)
-            for s in range(2):
-                s_send[d, c, s] = parts[s]
-            s_copy(c, d).start()
-
-        each(patch_peer, act)
-
-    send_spatial(0)
+    def send_spatial(c, d):
+        parts = pack_spatial(c, d)
+        for s in range(2):
+            s_send[d, c, s] = parts[s]
+        s_copy(c, d).start()
+
     for copy in loads[4:]:
         copy.wait()
 
@@ -195,8 +201,13 @@
             t_send[0, e, a] = parts[a]
         t_copy(e).start()
 
-    each(tm_peer, send_temporal)
-    send_spatial(1)
+    def both(j, carry):
+        send_spatial(0, patch_peer(j))
+        send_temporal(tm_peer(j))
+        return carry
+
+    lax.fori_loop(1, N, both, 0)
+    each(patch_peer, lambda d: send_spatial(1, d))
     for c in range(2):
         parts = pack_spatial(c, me_p)
         for s in range(2):
@@ -206,7 +217,7 @@
         t_in[me_t, a] = parts[a]
 
     def spatial(c):
-        each(patch_peer, lambda d: s_arrival(c, d).wait_recv())
+        s_all(c).wait_recv()
         low = lax.broadcasted_iota(jnp.int32, (QB, 128), 1) < 64
 
         def turn(i, carry):
@@ -246,13 +257,30 @@
             return carry
 
         lax.fori_loop(0, 1024 // QB, back, 0)
-        each(patch_peer, lambda d: b_copy(c, d).start())
+        def first(d, carry):
+            @pl.when(d != me_p)
+            def _():
+                b_copy(c, d).start()
+
+            return carry
+
+        def later(j, carry):
+            d = patch_peer(j)
+
+            @pl.when(d >= 4)
+            def _():
+                b_copy(c, d).start()
+
+            return carry
+
+        lax.fori_loop(0, 4, first, 0)
+        lax.fori_loop(1, N, later, 0)
         for s in range(2):
             s_back[me_p, c, s] = s_out[c, s, own_rows, :]
 
     def temporal():
         ws_copy.wait()
-        each(tm_peer, lambda e: t_arrival(e).wait_recv())
+        t_all().wait_recv()
 
         def widen(e, carry):
             for a in range(4):
@@ -342,12 +370,9 @@
         for a in range(4):
             outs[a][0, :, rows, cols] = t_back[e, a]
 
-    def take_temporal(e):
-        u_arrival(e).wait_recv()
-        unpack_temporal(e)
-
+    u_all().wait_recv()
     unpack_temporal(me_t)
-    each(tm_peer, take_temporal)
+    each(tm_peer, unpack_temporal)
 
     def unpack_spatial(d):
         f = d // 4
@@ -358,26 +383,18 @@
             high_ref[0, f, :, cols] = jnp.concatenate([x[:, 64:], y[:, 64:]], axis=1)
 
     unpack_spatial(me_p)
-    each(patch_peer, lambda d: b_arrival(0, d).wait_recv())
-
-    def drain_patch(d):
-        for c in range(2):
-            s_copy(c, d).wait_send()
-        b_copy(0, d).wait_send()
-
-    def drain_tm(e):
-        t_copy(e).wait_send()
-        u_copy(e).wait_send()
-
-    each(patch_peer, drain_patch)
-    each(tm_peer, drain_tm)
+    t_all().wait_send()
+    u_all().wait_send()
+    for c in range(2):
+        s_all(c).wait_send()
+    b_all(0).wait()
 
     def take_spatial(d):
-        b_arrival(1, d).wait_recv()
-        b_copy(1, d).wait_send()
+        b_arrival(d).wait_recv()
         unpack_spatial(d)
 
     each(patch_peer, take_spatial)
+    b_all(1).wait_send()
 
 
 def emit(*refs):
@@ -417,8 +434,7 @@
             pltpu.VMEM((N, 2, 2, PT, 128), BF16),
             pltpu.VMEM((N, 4, FR, 16, 128), BF16),
             dma, dma((2, 4)),
-            dma((2, N)), dma((2, N)), dma((N,)), dma((N,)),
-            dma((2, N)), dma((2, N)), dma((N,)), dma((N,)),
+            dma((2,)), dma((2,)), dma, dma, dma((2,)), dma, dma((N,)), dma, dma,
         ],
         compiler_params=pltpu.CompilerParams(
             collective_id=0, has_side_effects=True, vmem_limit_bytes=52900 << 10

time: 67 us -> 63 us (0.940)
  Pallas kernels: 65.6 us -> 61.5 us
    pallas_call x1, Pallas kernels: 64.2 us -> 60.1 us  [on_device(): pl.pallas_call(kernel, out_shape=(shape,) * 4, in_specs=[anywhere] * 5, o...]
where the time goes in v3:
time: 63 us; the launch traced here: 62.8 us
  Pallas kernels  61.5 us (98%)
  local copies, waits for them, and re-layouts  0.65 us (1%)
  between operations  0.65 us (1%)
    pallas_call x1, Pallas kernels, on_device(): pl.pallas_call(kernel, out_shape=(shape,) * 4, in_specs=[anywhere] * 5, o...  60.1 us
    pallas_call x1, Pallas kernels, on_device(): pl.pallas_call(emit, out_shape=(shape,) * 4, in_specs=[vmem] * 4, out_spe...  1.35 us

profile of v3, /device:TPU:1, one launch (start us, length us, event | category | flops | bytes accessed | tf_op | source)
XLA Modules:
  0.0 62.8 jit_solution(2082342082106847435)
XLA Ops:
  0.6 0.0 copy-start
  0.6 0.6 %copy-done = s32[64]{0:T(128)S(1)} copy-done((s32[64]{0:T(128)S(1)}, s32[64]{0:T(128)}, u32[]{:S(2)}) %copy-start) | copy-done | bytes 280
  1.3 60.1 %attention.1 = (bf16[1,4,64,1024]{3,2,1,0:T(8,128)(2,1)S(1)}, bf16[1,4,64,1024]{3,2,1,0:T(8,128)(2,1)S(1)}, bf16[1,4,64,1024]{3,2,1,0:T(8,128)(2,1)S(1)}, bf16[1,4,64,1024]{3,2,1,0:T(8,128)(2,1)S(1)}) custom-call(bf16[1,4,64,1024]{3,2,1,0:T(8,128)(2,1)} %q_hbm.1, bf16[1,4,64,1024]{3,2,1,0:T(8,128)(2,1)} %k_hbm.1, bf16[1,4,64,1024]{3,2,1,0:T(8,128)(2,1)} %v_hbm.1, ...), custom_call_target="tpu_custom_call" | custom-call | tf_op jit(solution)/shard_map/attention/pallas_call | solution.py:417
  61.4 1.3 %emit.1 = (bf16[1,4,64,1024]{3,2,1,0:T(8,128)(2,1)}, bf16[1,4,64,1024]{3,2,1,0:T(8,128)(2,1)}, bf16[1,4,64,1024]{3,2,1,0:T(8,128)(2,1)}, bf16[1,4,64,1024]{3,2,1,0:T(8,128)(2,1)}) custom-call(bf16[1,4,64,1024]{3,2,1,0:T(8,128)(2,1)S(1)} %get-tuple-element.8.refs_0_, bf16[1,4,64,1024]{3,2,1,0:T(8,128)(2,1)S(1)} %get-tuple-element.9.refs_1_, ...), custom_call_target="tpu_custom_call" | custom-call | tf_op jit(solution)/shard_map/emit/pallas_call | solution.py:444
Async XLA Ops:
  0.6 0.7 %copy-start = (s32[64]{0:T(128)S(1)}, s32[64]{0:T(128)}, u32[]{:S(2)}) copy-start(s32[64]{0:T(128)} %param.9) | copy-start | bytes 772

commit v4 on v3

--- a/solution.py
+++ b/solution.py
@@ -15,7 +15,7 @@
 PT = 64
 WINDOW = 16
 SCALE = 0.125
-GROUP = 4
+GROUP = 8
 QB = 256
 
 
@@ -55,15 +55,17 @@
 
     lax.fori_loop(1, N, greet, 0)
 
-    loads = []
     for half in range(2):
         for a, ref in enumerate((q_hbm, k_hbm, v_hbm, g_hbm)):
             cols = pl.ds(half * 512, 512)
             copy = pltpu.make_async_copy(
-                ref.at[0, :, :, cols], inp.at[a, :, :, cols], in_sem.at[half, a]
+                ref.at[0, :, :, cols], inp.at[a, :, :, cols], in_sem.at[half]
             )
             copy.start()
-            loads.append(copy)
+
+    def half_loaded(half):
+        cols = inp.at[:, :, :, pl.ds(half * 512, 512)]
+        return pltpu.make_async_copy(cols, cols, in_sem.at[half])
 
     ws_copy = pltpu.make_async_copy(ws_hbm, ws_ref, ws_sem)
     ws_copy.start()
@@ -177,8 +179,7 @@
 
         lax.fori_loop(1, N, body, 0)
 
-    for copy in loads[:4]:
-        copy.wait()
+    half_loaded(0).wait()
     pl.semaphore_wait(barrier, 2 * (N - 1))
 
     def send_spatial(c, d):
@@ -187,8 +188,7 @@
             s_send[d, c, s] = parts[s]
         s_copy(c, d).start()
 
-    for copy in loads[4:]:
-        copy.wait()
+    half_loaded(1).wait()
 
     def pack_temporal(e):
         rows = pl.ds(pl.multiple_of((e // 4) * 16, 16), 16)
@@ -414,6 +414,7 @@
     vmem = pl.BlockSpec(memory_space=pltpu.VMEM)
     dma = pltpu.SemaphoreType.DMA
     shape = jax.ShapeDtypeStruct((1, FR, PT, 1024), BF16)
+    inputs = (queries, key_vectors, value_vectors, grad_output, window_start.reshape(1, 64))
     results = pl.pallas_call(
         kernel,
         out_shape=(shape,) * 4,
@@ -433,14 +434,14 @@
             pltpu.VMEM((2, 2, 1024, 128), BF16),
             pltpu.VMEM((N, 2, 2, PT, 128), BF16),
             pltpu.VMEM((N, 4, FR, 16, 128), BF16),
-            dma, dma((2, 4)),
+            dma, dma((2,)),
             dma((2,)), dma((2,)), dma, dma, dma((2,)), dma, dma((N,)), dma, dma,
         ],
         compiler_params=pltpu.CompilerParams(
-            collective_id=0, has_side_effects=True, vmem_limit_bytes=52900 << 10
+            collective_id=0, has_side_effects=True, vmem_limit_bytes=48 << 20
         ),
         name="attention",
-    )(queries, key_vectors, value_vectors, grad_output, window_start.reshape(1, 64))
+    )(*(pltpu.with_memory_space_constraint(x, pltpu.HBM) for x in inputs))
     return pl.pallas_call(
         emit,
         out_shape=(shape,) * 4,
@@ -449,7 +450,7 @@
         scratch_shapes=[dma((4,))],
         compiler_params=pltpu.CompilerParams(vmem_limit_bytes=6 << 20),
         name="emit",
-    )(*results)
+    )(*(pltpu.with_memory_space_constraint(x, pltpu.VMEM) for x in results))
 
 
 def solution(mesh):

time: 63 us -> 62.5 us (level)
  local copies, waits for them, and re-layouts: 0.65 us -> 0 us
    unnamed x2 -> x0, local copies, waits for them, and re-layouts: 0.65 us -> none
where the time goes in v4:
time: 62.5 us; the launch traced here: 62.4 us
  Pallas kernels  61.8 us (99%)
  between operations  0.64 us (1%)
    pallas_call x1, Pallas kernels, on_device(): pl.pallas_call(kernel, out_shape=(shape,) * 4, in_specs=[anywhere] * 5, o...  60.4 us
    pallas_call x1, Pallas kernels, on_device(): pl.pallas_call(emit, out_shape=(shape,) * 4, in_specs=[vmem] * 4, out_spe...  1.35 us

profile of v4, /device:TPU:1, one launch (start us, length us, event | category | flops | bytes accessed | tf_op | source)
XLA Modules:
  0.0 62.4 jit_solution(4440992244320298580)
XLA Ops:
  0.6 60.4 %attention.1 = (bf16[1,4,64,1024]{3,2,1,0:T(8,128)(2,1)S(1)}, bf16[1,4,64,1024]{3,2,1,0:T(8,128)(2,1)S(1)}, bf16[1,4,64,1024]{3,2,1,0:T(8,128)(2,1)S(1)}, bf16[1,4,64,1024]{3,2,1,0:T(8,128)(2,1)S(1)}) custom-call(bf16[1,4,64,1024]{3,2,1,0:T(8,128)(2,1)} %q_hbm.1, bf16[1,4,64,1024]{3,2,1,0:T(8,128)(2,1)} %k_hbm.1, bf16[1,4,64,1024]{3,2,1,0:T(8,128)(2,1)} %v_hbm.1, ...), custom_call_target="tpu_custom_call" | custom-call | tf_op jit(solution)/shard_map/attention/pallas_call | solution.py:418
  61.1 1.3 %emit.1 = (bf16[1,4,64,1024]{3,2,1,0:T(8,128)(2,1)}, bf16[1,4,64,1024]{3,2,1,0:T(8,128)(2,1)}, bf16[1,4,64,1024]{3,2,1,0:T(8,128)(2,1)}, bf16[1,4,64,1024]{3,2,1,0:T(8,128)(2,1)}) custom-call(bf16[1,4,64,1024]{3,2,1,0:T(8,128)(2,1)S(1)} %get-tuple-element.8.refs_0_, bf16[1,4,64,1024]{3,2,1,0:T(8,128)(2,1)S(1)} %get-tuple-element.9.refs_1_, ...), custom_call_target="tpu_custom_call" | custom-call | tf_op jit(solution)/shard_map/emit/pallas_call | solution.py:445

commit v5 on v4

--- a/solution.py
+++ b/solution.py
@@ -16,7 +16,7 @@
 WINDOW = 16
 SCALE = 0.125
 GROUP = 8
-QB = 256
+QB = 512
 
 
 def dot(a, b, ca, cb):
@@ -239,8 +239,9 @@
             scores = dot(a_q, b, 1, 1)
             weight_grad = dot(a_g, b, 1, 1)
             e = jnp.exp(scores - jnp.max(scores, axis=1, keepdims=True))
-            w = e * (1.0 / jnp.sum(e, axis=1, keepdims=True))
-            delta = jnp.sum(w * weight_grad, axis=1, keepdims=True)
+            inverse = 1.0 / jnp.sum(e, axis=1, keepdims=True)
+            delta = jnp.sum(e * weight_grad, axis=1, keepdims=True) * inverse
+            w = e * inverse
             ds_b = (w * (weight_grad - delta)).astype(BF16)
             w_b = w.astype(BF16)
             out = jnp.where(low, dot(ds_b, b, 1, 0) * SCALE, dot(w_b, b, 1, 0))
@@ -267,13 +268,13 @@
         def later(j, carry):
             d = patch_peer(j)
 
-            @pl.when(d >= 4)
+            @pl.when(d >= 6)
             def _():
                 b_copy(c, d).start()
 
             return carry
 
-        lax.fori_loop(0, 4, first, 0)
+        lax.fori_loop(0, 6, first, 0)
         lax.fori_loop(1, N, later, 0)
         for s in range(2):
             s_back[me_p, c, s] = s_out[c, s, own_rows, :]

time: 62.5 us -> 62.7 us (level)
  no operation moved by 1% of the time
where the time goes in v5:
time: 62.7 us; the launch traced here: 62.6 us
  Pallas kernels  61.9 us (99%)
  between operations  0.64 us (1%)
    pallas_call x1, Pallas kernels, on_device(): pl.pallas_call(kernel, out_shape=(shape,) * 4, in_specs=[anywhere] * 5, o...  60.6 us
    pallas_call x1, Pallas kernels, on_device(): pl.pallas_call(emit, out_shape=(shape,) * 4, in_specs=[vmem] * 4, out_spe...  1.35 us

profile of v5, /device:TPU:1, one launch (start us, length us, event | category | flops | bytes accessed | tf_op | source)
XLA Modules:
  0.0 62.6 jit_solution(7594464196214768686)
XLA Ops:
  0.6 60.6 %attention.1 = (bf16[1,4,64,1024]{3,2,1,0:T(8,128)(2,1)S(1)}, bf16[1,4,64,1024]{3,2,1,0:T(8,128)(2,1)S(1)}, bf16[1,4,64,1024]{3,2,1,0:T(8,128)(2,1)S(1)}, bf16[1,4,64,1024]{3,2,1,0:T(8,128)(2,1)S(1)}) custom-call(bf16[1,4,64,1024]{3,2,1,0:T(8,128)(2,1)} %q_hbm.1, bf16[1,4,64,1024]{3,2,1,0:T(8,128)(2,1)} %k_hbm.1, bf16[1,4,64,1024]{3,2,1,0:T(8,128)(2,1)} %v_hbm.1, ...), custom_call_target="tpu_custom_call" | custom-call | tf_op jit(solution)/shard_map/attention/pallas_call | solution.py:419
  61.2 1.3 %emit.1 = (bf16[1,4,64,1024]{3,2,1,0:T(8,128)(2,1)}, bf16[1,4,64,1024]{3,2,1,0:T(8,128)(2,1)}, bf16[1,4,64,1024]{3,2,1,0:T(8,128)(2,1)}, bf16[1,4,64,1024]{3,2,1,0:T(8,128)(2,1)}) custom-call(bf16[1,4,64,1024]{3,2,1,0:T(8,128)(2,1)S(1)} %get-tuple-element.8.refs_0_, bf16[1,4,64,1024]{3,2,1,0:T(8,128)(2,1)S(1)} %get-tuple-element.9.refs_1_, ...), custom_call_target="tpu_custom_call" | custom-call | tf_op jit(solution)/shard_map/emit/pallas_call | solution.py:446
